TPU v7x, 32 devices: a whole 2x2x4 slice. The times are simulated.
32 devices in a mesh: grp: 2 (over core), pts: 16 (over z, y, x).
Axes of the slice: x: 2, y: 2, z: 4, core: 2. Of those that a mesh axis runs over, the one named last changes fastest.
Arguments:
- element_attribute_table: bfloat16 [262144, 512], P(('grp', 'pts')), parts along dimension 0, may hold values from -6 to 6
- active_group_tally: int32 [32], P(('grp', 'pts')), parts along dimension 0, may hold values from 48 to 64, as said below
- group_destination_part: int32 [2048], P(('grp', 'pts')), parts along dimension 0, may hold values from 0 to 15, as said below
- element_vertex_permutation: int32 [2048, 128], P(('grp', 'pts')), parts along dimension 0, may hold values from 0 to 127, each once within a row
- softness_factor: float32 [8], replicated, may hold values from 0.15 to 0.6
- entry_projection_coefficients: bfloat16 [512, 1024], replicated, may hold values from -0.25 to 0.25
- partition_score_coefficients: bfloat16 [8, 64, 256], replicated, may hold values from -0.75 to 0.75
- summary_query_key_coefficients: bfloat16 [64, 192], replicated, may hold values from -0.75 to 0.75
- final_projection_coefficients: bfloat16 [512, 512], replicated, may hold values from -0.25 to 0.25
Outputs:
- point_features: bfloat16 [262144, 512], P(('grp', 'pts')), parts along dimension 0
There are 2 independent parts, one for each index of `grp`. A program takes and returns all parts, laid end to end along the dimension named above; an argument that names none is the same for every part. Nothing has to cross between parts.
Inputs may be any that keep to these rules, and one draw needn't show every extreme that they name: The live blocks of a device are its first active_group_tally slots; some device has all 64 live. `group_destination_part`: no device names a point shard in more than 4 of its slots; some point shard is named exactly 4 times by the live blocks of every device. `element_vertex_permutation`: each row is a permutation.
All inputs are finite; a program needn't handle non-finite values.
Results may differ from a plain program's by a relative error of at most 0.0016.
Values may be sent and summed in bfloat16 or wider, within the bound.
No kernel may reach another device: no remote copies, remote signals or barrier semaphores. Data moves between devices by JAX's collectives and lax.ppermute only.
A program may use at most 192 MiB of HBM per device.

v0:
```python
import functools
import math

import jax
import jax.numpy as jnp
from jax import lax
from jax.experimental import pallas as pl
from jax.experimental.pallas import tpu as pltpu
from jax.sharding import PartitionSpec as P

NORM_EPS = 1e-05
SLICE_EPS = 1e-05
LOG2E = math.log2(math.e)
MIB = 1 << 20
EXACT = lax.Precision.HIGHEST
ANY = pl.BlockSpec(memory_space=pl.ANY)
SMEM = pl.BlockSpec(memory_space=pltpu.SMEM)
VMEM = pl.BlockSpec(memory_space=pltpu.VMEM)
HIDDEN = pl.CostEstimate(flops=0, bytes_accessed=0, transcendentals=0)


def dot(a, b, contract, precision=None):
    return lax.dot_general(
        a, b, (contract, ((), ())), preferred_element_type=jnp.float32, precision=precision
    )


def normalize_rows(point_rows):
    values = point_rows.astype(jnp.float32)
    centre = jnp.mean(values, axis=-1, keepdims=True)
    values = values - centre
    spread = jnp.mean(jnp.square(values), axis=-1, keepdims=True)
    return (values * lax.rsqrt(spread + NORM_EPS)).astype(jnp.bfloat16)


def passing(carried, first_input, first_output):
    shapes = [pltpu.HBM(a.shape, a.dtype) for a in carried]
    aliases = {first_input + i: first_output + i for i in range(len(carried))}
    return [ANY] * len(carried), shapes, aliases


def plan_slots(per_peer, tally_ref, part_ref, slots_ref, counts_ref):
    shards = counts_ref.shape[0]

    @pl.loop(0, shards)
    def _(p):
        counts_ref[p] = 0
        for q in range(per_peer):
            slots_ref[p * per_peer + q] = 0

    @pl.loop(0, tally_ref[0])
    def _(b):
        part = part_ref[b]
        at = counts_ref[part]
        slots_ref[part * per_peer + jnp.minimum(at, per_peer - 1)] = b
        counts_ref[part] = at + 1


def gather_kernel(plan, offsets, per_peer, rows, here_ref, *refs):
    count = len(offsets)
    *refs, taken, made, in_sem, out_sem = refs
    outs = refs[-count:]
    if plan:
        tally_ref, part_ref, perm_ref, table_ref, slots_ref, counts_ref = refs[:6]
        plan_slots(per_peer, tally_ref, part_ref, slots_ref, counts_ref)
    else:
        slots_ref, perm_ref, table_ref = refs[:3]

    def block(j, q):
        return slots_ref[(here_ref[0] ^ offsets[j]) * per_peer + q]

    def fetch(j, q):
        return pltpu.make_async_copy(
            table_ref.at[block(j, q)], taken.at[j, q], in_sem.at[j, q]
        )

    def store(j):
        return pltpu.make_async_copy(made.at[j], outs[j], out_sem.at[j])

    for j in range(count):

        @pl.loop(0, per_peer)
        def _(q):
            fetch(j, q).start()

    for j in range(count):

        @pl.loop(0, per_peer)
        def _(q):
            fetch(j, q).wait()
            wanted = perm_ref[pl.ds(block(j, q), 1), :]
            level = lax.broadcasted_iota(jnp.int32, (rows, rows), 0)
            picking = jnp.where(level == wanted, 1.0, 0.0).astype(jnp.bfloat16)
            made[j, pl.ds(pl.multiple_of(q * rows, rows), rows), :] = dot(
                picking, taken[j, q], ((0,), (0,))
            ).astype(jnp.bfloat16)

        store(j).start()
    for j in range(count):
        store(j).wait()


def gather_blocks(here, slots, perm, table, offsets, per_peer, carried=(), shards=0):
    count = len(offsets)
    blocks, rows = perm.shape
    channels = table.shape[-1]
    plan = len(slots) > 1
    specs, shapes, aliases = passing(carried, 3 + len(slots), 0)
    planned = [
        jax.ShapeDtypeStruct((shards * per_peer,), jnp.int32),
        jax.ShapeDtypeStruct((shards,), jnp.int32),
    ] * plan
    out = pl.pallas_call(
        functools.partial(gather_kernel, plan, offsets, per_peer, rows),
        out_shape=shapes + planned + [pltpu.HBM((per_peer * rows, channels), jnp.bfloat16)] * count,
        in_specs=[SMEM] * (1 + len(slots)) + [VMEM, ANY] + specs,
        out_specs=specs + [SMEM] * len(planned) + [ANY] * count,
        input_output_aliases=aliases,
        scratch_shapes=[
            pltpu.VMEM((count, per_peer, rows, channels), jnp.bfloat16),
            pltpu.VMEM((count, per_peer * rows, channels), jnp.bfloat16),
            pltpu.SemaphoreType.DMA((count, per_peer)),
            pltpu.SemaphoreType.DMA((count,)),
        ],
        compiler_params=pltpu.CompilerParams(vmem_limit_bytes=48 * MIB),
        cost_estimate=HIDDEN,
        name="gather_blocks",
    )(here, *slots, perm, table.reshape(blocks, rows, channels), *carried)
    return out[len(carried) :], out[: len(carried)]


def slice_powers(raw_scores, factor):
    scaled = raw_scores * factor
    return jnp.exp2(scaled - jnp.max(scaled, axis=0, keepdims=True))


def head_scores(middle, score_ref):
    heads, _, width = score_ref.shape
    made = [dot(score_ref[h], middle[h * width : (h + 1) * width], ((1,), (0,))) for h in range(1)]
    for h in range(heads):
        if h + 1 < heads:
            made.append(
                dot(score_ref[h + 1], middle[(h + 1) * width : (h + 2) * width], ((1,), (0,)))
            )
        yield h, made[h]


def summary_kernel(
    pieces, start, passed, seat_ref, live_ref, factor_ref, before_ref, tail_ref, rows_ref, entry_ref, score_ref, *refs
):
    out_refs, total = refs[passed : passed + pieces], refs[-1]
    heads, slices, width = score_ref.shape
    tile = rows_ref.shape[0]
    step = pl.program_id(0)
    channels = heads * width
    height = total.shape[1]

    @pl.when(step == 0)
    def _():
        total[...] = before_ref[...] if start else jnp.zeros_like(total)

    left = live_ref[0] - (start + step) * tile

    @pl.when(left > 0)
    def _():
        normed = normalize_rows(rows_ref[...])
        middle = dot(entry_ref[channels:, :], normed, ((1,), (1,))).astype(jnp.bfloat16)
        features = dot(entry_ref[:channels, :], normed, ((1,), (1,)))
        alive = lax.broadcasted_iota(jnp.int32, (1, tile), 1) < left
        for h, scores in head_scores(middle, score_ref):
            span = slice(h * width, (h + 1) * width)
            powers = slice_powers(scores, factor_ref[h])
            share = jnp.where(alive, 1.0 / jnp.sum(powers, axis=0, keepdims=True), 0.0)
            terms = jnp.concatenate(
                [features[span] * share, jnp.broadcast_to(share, (height - width, tile))], axis=0
            ).astype(jnp.bfloat16)
            total[h] += dot(terms, powers.astype(jnp.bfloat16), ((1,), (1,)))

    @pl.when(step == pl.num_programs(0) - 1)
    def _():
        if not pieces:
            refs[passed][...] = total[...]
        share = heads // max(pieces, 1)
        level = lax.broadcasted_iota(jnp.int32, (height - width, slices), 0)
        for p in range(pieces):
            for i in range(share):
                part = total[(seat_ref[0] ^ p) * share + i]
                rest = jnp.where(level == 0, part[width:], tail_ref[...])
                out_refs[p][i, :width] = part[:width].astype(jnp.bfloat16)
                out_refs[p][i, width:] = rest.astype(jnp.bfloat16)


def summarize(
    seat, live_rows, factors, before, tail, table, entry_t, score_t, steps, pieces, carried=()
):
    heads, slices, width = score_t.shape
    total_rows, channels = table.shape
    tile = total_rows // steps[2]
    whole = jax.ShapeDtypeStruct((heads, width + tail.shape[0], slices), jnp.float32)
    specs, shapes, aliases = passing(carried, 8, 0)
    outs = [jax.ShapeDtypeStruct((heads // max(pieces, 1),) + whole.shape[1:], jnp.bfloat16)]
    outs = outs * pieces or [whole]
    out = pl.pallas_call(
        functools.partial(summary_kernel, pieces, steps[0], 2 * len(carried)),
        grid=(steps[1] - steps[0],),
        out_shape=shapes + outs,
        in_specs=[
            SMEM,
            SMEM,
            SMEM,
            pl.BlockSpec(before.shape, lambda i: (0,) * before.ndim),
            pl.BlockSpec(tail.shape, lambda i: (0, 0)),
            pl.BlockSpec((tile, channels), lambda i: (steps[0] + i, 0)),
            pl.BlockSpec(entry_t.shape, lambda i: (0, 0)),
            pl.BlockSpec(score_t.shape, lambda i: (0, 0, 0)),
        ]
        + specs,
        out_specs=specs + [pl.BlockSpec(o.shape, lambda i: (0, 0, 0)) for o in outs],
        scratch_shapes=[pltpu.VMEM(whole.shape, jnp.float32)],
        input_output_aliases=aliases,
        compiler_params=pltpu.CompilerParams(vmem_limit_bytes=40 * MIB),
        cost_estimate=HIDDEN,
        name="summarize",
    )(
        seat,
        live_rows,
        factors,
        before,
        tail,
        pltpu.with_memory_space_constraint(table, pltpu.HBM),
        entry_t,
        score_t,
        *carried,
    )
    return out[len(carried) :], out[: len(carried)]


def small_call(kernel, name, inputs, shapes, carried, scalars=0, **kwargs):
    specs, passed, aliases = passing(carried, len(inputs), 0)
    out = pl.pallas_call(
        functools.partial(kernel, **kwargs),
        out_shape=passed + shapes,
        in_specs=[SMEM] * scalars + [VMEM] * (len(inputs) - scalars) + specs,
        out_specs=specs + [VMEM] * len(shapes),
        input_output_aliases=aliases,
        compiler_params=pltpu.CompilerParams(vmem_limit_bytes=16 * MIB),
        cost_estimate=HIDDEN,
        name=name,
    )(*inputs, *carried)
    return out[len(carried) :], out[: len(carried)]


def total_of(refs, *at):
    total = refs[0][at].astype(jnp.float32)
    for ref in refs[1:]:
        total += ref[at].astype(jnp.float32)
    return total


def add_kernel(*refs, parts):
    refs[-1][...] = total_of(refs[:parts], Ellipsis).astype(refs[-1].dtype)


def attend_kernel(*refs, parts):
    maps_ref, sums, out_ref, tail_ref = refs[0], refs[1 : 1 + parts], refs[-2], refs[-1]
    heads, width, slices = out_ref.shape
    maps = maps_ref[...].astype(jnp.float32)
    for h in range(heads):
        total = total_of(sums, h)
        tokens = total[:width] / (total[width : width + 1] + SLICE_EPS)
        project = dot(maps, tokens, ((1,), (0,)), EXACT)
        queries, keys, values = (project[i * width : (i + 1) * width] for i in range(3))
        scores = dot(keys, queries, ((0,), (0,)), EXACT) * width**-0.5
        powers = jnp.exp(scores - jnp.max(scores, axis=0, keepdims=True))
        mixed = dot(values, powers, ((1,), (0,)), EXACT)
        out_ref[h] = (mixed / jnp.sum(powers, axis=0, keepdims=True)).astype(jnp.bfloat16)
        if h == 0:
            tail_ref[...] = total[width:]


def join_kernel(seat_ref, *refs, parts):
    out_ref = refs[-1]
    share = refs[0].shape[0]
    for p in range(parts):
        out_ref[pl.ds((seat_ref[0] ^ p) * share, share)] = refs[p][...]


def entry_of(ids, chunk):
    rank = ids[0]
    for i, other in enumerate(ids[1:]):
        rank = jnp.where(chunk == i + 1, other, rank)
    return rank


def finish_kernel(ids, block_rows, extra, place_ref, valid_ref, factor_ref, *refs):
    chunks = len(ids)
    xs = refs[:chunks]
    entry_ref, score_ref, mixed_ref, final_ref = refs[chunks : chunks + 4]
    out_ref, held = refs[chunks + 4 + extra], refs[-1]
    heads, slices, width = score_ref.shape
    tile = held.shape[0]
    chunk, step = pl.program_id(0), pl.program_id(1)
    for i in range(chunks):

        @pl.when(chunk == i)
        def _():
            held[...] = xs[i][...]

    left = valid_ref[place_ref[entry_of(ids, chunk)]] * block_rows - step * tile

    @pl.when(left <= 0)
    def _():
        out_ref[...] = jnp.zeros_like(out_ref)

    @pl.when(left > 0)
    def _():
        rows = held[...]
        normed = normalize_rows(rows)
        middle = dot(entry_ref[...], normed, ((1,), (1,))).astype(jnp.bfloat16)
        spread = []
        for h, scores in head_scores(middle, score_ref):
            powers = slice_powers(scores, factor_ref[h])
            share = 1.0 / jnp.sum(powers, axis=0, keepdims=True)
            back = dot(mixed_ref[h], powers.astype(jnp.bfloat16), ((1,), (0,)))
            spread.append((back * share).astype(jnp.bfloat16))
        spread = jnp.concatenate(spread, axis=0)
        update = dot(spread, final_ref[...], ((0,), (0,)))
        done = rows.astype(jnp.float32) + update
        alive = lax.broadcasted_iota(jnp.int32, (tile, 1), 0) < left
        out_ref[...] = jnp.where(alive, done, 0.0).astype(out_ref.dtype)


def finish(
    ids, block_rows, place, valid, factors, xs, entry_t, score_t, mixed, final, out, total_rows, carried=(), tile=512
):
    heads, slices, width = score_t.shape
    chunk_rows, channels = xs[0].shape
    tile = min(tile, chunk_rows)
    tiles = chunk_rows // tile
    chunks = len(xs)

    def chunk_spec(i):
        def index(j, t, *_):
            return jnp.where(j == i, t, jnp.where(j < i, 0, tiles - 1)), 0

        return pl.BlockSpec((tile, channels), index)

    def whole(a):
        return pl.BlockSpec(a.shape, lambda *_: (0,) * a.ndim)

    kept = list(carried) + ([] if out is None else [out])
    specs, shapes, aliases = passing(kept, 3 + chunks + 4, 0)
    if out is None:
        shapes = shapes + [jax.ShapeDtypeStruct((total_rows, channels), jnp.bfloat16)]
    out_specs = [ANY] * (len(shapes) - 1) + [
        pl.BlockSpec((tile, channels), lambda j, t, place, *_: (place[entry_of(ids, j)] * tiles + t, 0))
    ]
    work = chunks * chunk_rows
    result = pl.pallas_call(
        functools.partial(finish_kernel, ids, block_rows, len(kept) + len(shapes) - 1),
        out_shape=shapes,
        grid_spec=pltpu.PrefetchScalarGridSpec(
            num_scalar_prefetch=3,
            grid=(chunks, tiles),
            in_specs=[chunk_spec(i) for i in range(chunks)]
            + [whole(entry_t), whole(score_t), whole(mixed), whole(final)]
            + specs,
            out_specs=out_specs,
            scratch_shapes=[pltpu.VMEM((tile, channels), jnp.bfloat16)],
        ),
        input_output_aliases=aliases,
        compiler_params=pltpu.CompilerParams(vmem_limit_bytes=48 * MIB),
        cost_estimate=HIDDEN,
        name="finish",
    )(
        place,
        valid,
        factors,
        *(pltpu.with_memory_space_constraint(x, pltpu.HBM) for x in xs),
        entry_t,
        score_t,
        mixed,
        final,
        *kept,
    )
    return result[-1], result[:-1]


def per_device(
    element_attribute_table,
    active_group_tally,
    group_destination_part,
    element_vertex_permutation,
    softness_factor,
    entry_projection_coefficients,
    partition_score_coefficients,
    summary_query_key_coefficients,
    final_projection_coefficients,
):
    block_count, block_rows = element_vertex_permutation.shape
    total_rows, channels = element_attribute_table.shape
    heads, width, slices = partition_score_coefficients.shape
    shards = lax.axis_size("pts")
    here = lax.axis_index("pts")
    per_peer = max(1, (block_count + shards - 1) // shards)
    chunk_rows = per_peer * block_rows

    inner = 1 << (shards.bit_length() // 2)
    assert shards & (shards - 1) == 0 and heads % inner == 0
    outer = shards // inner

    def send(chunk, k):
        return lax.ppermute(chunk, "pts", [(i, i ^ k) for i in range(shards)])

    far = list(range(shards // 2, shards))
    near = list(range(1, shards // 2))
    first, second = far[:1], far[1:3]
    late = [far[6 + i : 7 + i] + near[3 + 2 * i : 5 + 2 * i] for i in range(len(far) - 6)]
    third = near[:2] + far[3:5] + far[5:6] + near[2:3] + [k for wave in late for k in wave] + [0]
    ranks = first + second + third
    groups = [[0] + far[:2], far[2:3] + near[:2], far[3:4] + near[2:3]]
    groups += [far[4 + i : 5 + i] + near[3 + 2 * i : 5 + 2 * i] for i in range(len(far) - 4)]

    factors = LOG2E / softness_factor
    entry_t = entry_projection_coefficients.T
    score_t = partition_score_coefficients.transpose(0, 2, 1)
    maps_t = summary_query_key_coefficients.T

    arrived = {}
    held = {}
    at_here = here[None]
    blocks = (element_vertex_permutation, element_attribute_table)

    def gather(offsets, order):
        chunks, (order,) = gather_blocks(at_here, (slots,), *blocks, offsets, per_peer, (order,))
        held.update(zip(offsets, chunks))
        return order

    def depart(wave):
        for k in wave:
            arrived[k] = send(held.pop(k), k)

    def carry(order, *offsets):
        return (order,) + tuple(held.values()) + tuple(arrived[k] for k in offsets)

    def release(carried, wave, *offsets):
        held.update(zip(list(held), carried[1:]))
        arrived.update(zip(offsets, carried[1 + len(held) :]))
        depart(wave)
        return carried[0]

    places = (active_group_tally, group_destination_part)
    (slots, counts, *chunks), _ = gather_blocks(
        at_here, places, *blocks, first, per_peer, shards=shards
    )
    held.update(zip(first, chunks))
    depart(first)
    order = gather(second, jnp.zeros((8, 128), jnp.int32))
    depart(second[:1])

    seat = (here % inner)[None]
    rows = -(-shards * shards // slices)
    height = -(-(width + 1 + rows) // 16) * 16
    tail = jnp.where(jnp.arange(shards)[:, None] == here, counts[None, :], 0).reshape(rows, slices)
    tail = jnp.pad(tail.astype(jnp.float32), ((1, height - width - 1 - rows), (0, 0)))
    live_rows = active_group_tally * block_rows
    weights = (tail, element_attribute_table, entry_t, score_t)
    steps = 8
    nothing = jnp.zeros((8, 128))
    (begun,), carried = summarize(
        seat, live_rows, factors, nothing, *weights, (0, steps - 1, steps), 0, carry(order)
    )
    order = release(carried, second[1:2])
    pieces, carried = summarize(
        seat, live_rows, factors, begun, *weights, (steps - 1, steps, steps), inner, carry(order, far[0])
    )
    order = release(carried, [], far[0])
    parts = [pieces[0]] + [send(pieces[k], k) for k in range(1, inner)]
    piece = jax.ShapeDtypeStruct(parts[0].shape, jnp.bfloat16)
    (part,), carried = small_call(
        add_kernel, "add", parts, [piece], carry(order, far[1]), parts=inner
    )
    order = release(carried, [], far[1])
    parts = [part] + [send(part, k * inner) for k in range(1, outer)]
    order = gather(third, order)
    arrived[0] = held.pop(0)
    depart(third[:2])
    mixed = jax.ShapeDtypeStruct((heads // inner, width, slices), jnp.bfloat16)
    (mixed, tails), carried = small_call(
        attend_kernel,
        "attend",
        [maps_t] + parts,
        [mixed, jax.ShapeDtypeStruct(tail.shape, jnp.float32)],
        carry(order, far[2]),
        parts=outer,
    )
    order = release(carried, third[2:4], far[2])
    received = tails[1 : 1 + rows].reshape(shards, shards)[:, here].astype(jnp.int32)
    parts = [mixed] + [send(mixed, k) for k in range(1, inner)]
    mixed = jax.ShapeDtypeStruct((heads, width, slices), jnp.bfloat16)
    (mixed,), carried = small_call(
        join_kernel, "join", [seat] + parts, [mixed], carry(order), scalars=1, parts=inner
    )
    order = release(carried, third[4:6])

    middle_t = entry_t[channels:]
    sources = here ^ jnp.array(ranks, jnp.int32)
    out = None
    for i, group in enumerate(groups):
        out, carried = finish(
            [ranks.index(k) for k in group],
            block_rows,
            sources,
            received,
            factors,
            [arrived[k] for k in group],
            middle_t,
            score_t,
            mixed,
            final_projection_coefficients,
            out,
            shards * chunk_rows,
            carry(order),
        )
        order = release(carried, late[i] if i < len(late) else [])
    return out


def solution(mesh):
    placed = (
        P(("grp", "pts"), None),
        P(("grp", "pts")),
        P(("grp", "pts")),
        P(("grp", "pts"), None),
        P(),
        P(),
        P(),
        P(),
        P(),
    )
    return jax.shard_map(
        per_device, mesh=mesh, in_specs=placed, out_specs=P(("grp", "pts"), None), check_vma=False
    )
```

profile of v0, /device:TPU:8, one launch (start us, length us, event | category | flops | bytes accessed | tf_op | source)
XLA Modules:
  0.0 229.2 jit_solution(1951721276228657741)
XLA Ops:
  0.7 0.7 copy-done.1
  2.1 4.7 %gather_blocks.3 = (s32[64]{0:T(128)S(1)}, s32[16]{0:T(128)S(1)}, bf16[512,512]{1,0:T(8,128)(2,1)}) custom-call(s32[1]{0:T(128)} %bitcast.2.here_ref, s32[1]{0:T(128)S(6)} %copy.119.refs_0_, s32[64]{0:T(128)S(1)} %copy-done.3, s32[64,128]{1,0:T(8,128)S(1)} %copy-done.1, bf16[64,128,512]{2,1,0:T(8,128)(2,1)} %bitcast.27), custom_call_target="tpu_custom_call" | custom-call | tf_op jit(solution)/shard_map/gather_blocks/pallas_call | solution.py:113
  6.8 2.8 %collective-permute-start = (bf16[512,512]{1,0:T(8,128)(2,1)}, bf16[512,512]{1,0:T(8,128)(2,1)S(1)}, u32[]{:S(2)}, u32[]{:S(2)}) collective-permute-start(bf16[512,512]{1,0:T(8,128)(2,1)} %get-tuple-element.89), channel_id=1, source_target_pairs={{0,8},{1,9},{2,10},{3,11},{4,12},{5,13},{6,14},{7,15},{8,0},{9,1},... | collective-permute-start | bytes 1572872 | tf_op jit(solution)/shard_map/ppermute | solution.py:413
  10.2 4.2 %gather_blocks.4 = (s32[8,128]{1,0:T(8,128)}, bf16[512,512]{1,0:T(8,128)(2,1)}, bf16[512,512]{1,0:T(8,128)(2,1)}) custom-call(s32[1]{0:T(128)} %bitcast.2.here_ref, s32[64]{0:T(128)S(1)} %get-tuple-element.84.refs_0_, s32[64,128]{1,0:T(8,128)S(1)} %copy-done.2, bf16[64,128,512]{2,1,0:T(8,128)(2,1)} %bitcast.28, ...), custom_call_target="tpu_custom_call", output_to_operand_aliasing={{0}: (4, {})} | custom-call | tf_op jit(solution)/shard_map/gather_blocks/pallas_call | solution.py:113
  14.3 1.3 collective-permute-start.4
  16.7 31.3 %summarize.2 = (s32[8,128]{1,0:T(8,128)}, bf16[512,512]{1,0:T(8,128)(2,1)}, f32[8,80,256]{2,1,0:T(8,128)S(1)}) custom-call(s32[1]{0:T(128)} %bitcast.1.seat_ref, s32[1]{0:T(128)S(6)} %mul.3.live_ref, f32[8]{0:T(128)S(1)} %broadcast_divide_fusion.factor_ref, f32[8,128]{1,0:T(8,128)S(1)} %broadcast_in_dim.35.before_ref, ...), custom_call_target="tpu_custom_call", output_to_operand_aliasing={{0}: (8, {}), {1}: (9, {})} | custom-call | tf_op jit(solution)/shard_map/summarize/pallas_call | solution.py:203
  48.0 3.6 %collective-permute-start.8 = (bf16[512,512]{1,0:T(8,128)(2,1)}, bf16[512,512]{1,0:T(8,128)(2,1)S(1)}, u32[]{:S(2)}, u32[]{:S(2)}) collective-permute-start(bf16[512,512]{1,0:T(8,128)(2,1)} %get-tuple-element.109), channel_id=1, source_target_pairs={{0,10},{1,11},{2,8},{3,9},{4,14},{5,15},{6,12},{7,13},{8,2},{9,3},... | collective-permute-start | bytes 1572872 | tf_op jit(solution)/shard_map/ppermute | solution.py:413
  51.6 0.8 copy-done.5
  52.4 1.5 summarize.3
  53.9 4.7 %collective-permute-start.1 = (bf16[2,80,256]{2,1,0:T(8,128)(2,1)S(1)}, bf16[2,80,256]{2,1,0:T(8,128)(2,1)S(1)}, u32[]{:S(2)}, u32[]{:S(2)}) collective-permute-start(bf16[2,80,256]{2,1,0:T(8,128)(2,1)S(1)} %get-tuple-element.91), channel_id=1, source_target_pairs={{0,1},{1,0},{2,3},{3,2},{4,5},{5,4},{6,7},{7,6},{8,9},{9,8},{10,11... | collective-permute-start | bytes 245768 | tf_op jit(solution)/shard_map/ppermute | solution.py:413
  58.7 1.5 collective-permute-start.3
  60.2 5.6 %collective-permute-done.4.refs_5_ = bf16[512,512]{1,0:T(8,128)(2,1)} collective-permute-done((bf16[512,512]{1,0:T(8,128)(2,1)}, bf16[512,512]{1,0:T(8,128)(2,1)}, u32[]{:S(2)}, u32[]{:S(2)}) %collective-permute-start.4) | collective-permute-done | bytes 524320 | tf_op jit(solution)/shard_map/ppermute | solution.py:413
  65.8 0.9 collective-permute-done.2.refs_2_
  66.8 14.4 %gather_blocks.5 = (s32[8,128]{1,0:T(8,128)}, bf16[512,512]{1,0:T(8,128)(2,1)}, bf16[512,512]{1,0:T(8,128)(2,1)}, bf16[512,512]{1,0:T(8,128)(2,1)}, bf16[512,512...) custom-call(s32[1]{0:T(128)} %bitcast.2.here_ref, ...), custom_call_target="tpu_custom_call", output_to_operand_aliasing={{0}: (4, {})} | custom-call | tf_op jit(solution)/shard_map/gather_blocks/pallas_call | solution.py:113
  81.2 0.8 collective-permute-start.9
  82.0 1.4 collective-permute-start.10
  83.4 1.5 collective-permute-start.7
  84.9 3.3 %collective-permute-start.6 = (bf16[2,80,256]{2,1,0:T(8,128)(2,1)S(1)}, bf16[2,80,256]{2,1,0:T(8,128)(2,1)S(1)}, u32[]{:S(2)}, u32[]{:S(2)}) collective-permute-start(bf16[2,80,256]{2,1,0:T(8,128)(2,1)S(1)} %get-tuple-element.96.refs_1_), channel_id=1, source_target_pairs={{0,8},{1,9},{2,10},{3,11},{4,12},{5,13},{6,14},{7,15},{8,0},{9,1},... | collective-permute-start | bytes 245768 | tf_op jit(solution)/shard_map/ppermute | solution.py:413
  89.7 2.7 %collective-permute-done.6.refs_3_ = bf16[2,80,256]{2,1,0:T(8,128)(2,1)S(1)} collective-permute-done((bf16[2,80,256]{2,1,0:T(8,128)(2,1)S(1)}, bf16[2,80,256]{2,1,0:T(8,128)(2,1)S(1)}, u32[]{:S(2)}, u32[]{:S(2)}) %collective-permute-start.6) | collective-permute-done | bytes 81952 | tf_op jit(solution)/shard_map/ppermute | solution.py:413
  92.3 1.2 collective-permute-done.5.refs_2_
  93.5 2.3 %attend.1 = (s32[8,128]{1,0:T(8,128)}, bf16[512,512]{1,0:T(8,128)(2,1)}, bf16[512,512]{1,0:T(8,128)(2,1)}, bf16[512,512]{1,0:T(8,128)(2,1)}, bf16[512,512]{1,0:T...) custom-call(bf16[192,64]{1,0:T(8,128)(2,1)S(1)} %bitcast.19, ...), custom_call_target="tpu_custom_call", output_to_operand_aliasing={{0}: (5, {}), {1}: (6, {}), {2}: (7, {}), {3}: (8, {}), {4}... | custom-call | tf_op jit(solution)/shard_map/attend/pallas_call | solution.py:240
  95.8 1.4 collective-permute-start.13
  97.3 1.5 collective-permute-start.12
  99.6 1.4 collective-permute-done.13.refs_3_
  101.1 0.7 collective-permute-start.19
  101.8 4.1 %collective-permute-start.22 = (bf16[512,512]{1,0:T(8,128)(2,1)}, bf16[512,512]{1,0:T(8,128)(2,1)S(1)}, u32[]{:S(2)}, u32[]{:S(2)}) collective-permute-start(bf16[512,512]{1,0:T(8,128)(2,1)} %get-tuple-element.148), channel_id=1, source_target_pairs={{0,11},{1,10},{2,9},{3,8},{4,15},{5,14},{6,13},{7,12},{8,3},{9,2},... | collective-permute-start | bytes 1572872 | tf_op jit(solution)/shard_map/ppermute | solution.py:413
  105.9 1.3 collective-permute-start.23
  107.2 10.1 %finish.7 = (s32[8,128]{1,0:T(8,128)}, bf16[512,512]{1,0:T(8,128)(2,1)}, bf16[512,512]{1,0:T(8,128)(2,1)}, bf16[512,512]{1,0:T(8,128)(2,1)}, bf16[512,512]{1,0:T...) custom-call(s32[16]{0:T(128)S(1)} %broadcast_xor_fusion.place_ref, ...), custom_call_target="tpu_custom_call", output_to_operand_aliasing={{0}: (10, {}), {1}: (11, {}), {2}: (12, {}), {3}: (13, {}),... | custom-call | tf_op jit(solution)/shard_map/finish/pallas_call | solution.py:359
  117.5 2.8 %collective-permute-start.21 = (bf16[512,512]{1,0:T(8,128)(2,1)}, bf16[512,512]{1,0:T(8,128)(2,1)S(1)}, u32[]{:S(2)}, u32[]{:S(2)}) collective-permute-start(bf16[512,512]{1,0:T(8,128)(2,1)} %get-tuple-element.147), channel_id=1, source_target_pairs={{0,5},{1,4},{2,7},{3,6},{4,1},{5,0},{6,3},{7,2},{8,13},{9,12},{10,... | collective-permute-start | bytes 1572872 | tf_op jit(solution)/shard_map/ppermute | solution.py:413
  120.3 10.1 %finish.8 = (s32[8,128]{1,0:T(8,128)}, bf16[512,512]{1,0:T(8,128)(2,1)}, bf16[512,512]{1,0:T(8,128)(2,1)}, bf16[512,512]{1,0:T(8,128)(2,1)}, bf16[8192,512]{1,0:T(8,128)(2,1)}) custom-call(s32[16]{0:T(128)S(1)} %broadcast_xor_fusion.place_ref, s32[16]{0:T(128)S(1)} %bitcast.21, ...), custom_call_target="tpu_custom_call", output_to_operand_aliasing={{0}: (10, {}), {1}: (11, {}), {2}: (12, {}), {3}: (13, {}),... | custom-call | tf_op jit(solution)/shard_map/finish/pallas_call | solution.py:359
  130.4 7.2 %collective-permute-done.19.refs_0_ = bf16[512,512]{1,0:T(8,128)(2,1)S(1)} collective-permute-done((bf16[512,512]{1,0:T(8,128)(2,1)}, bf16[512,512]{1,0:T(8,128)(2,1)S(1)}, u32[]{:S(2)}, u32[]{:S(2)}) %collective-permute-start.19) | collective-permute-done | bytes 524320 | tf_op jit(solution)/shard_map/ppermute | solution.py:413
  137.6 1.5 collective-permute-start.16
  139.0 11.1 %collective-permute-done.22.refs_0_ = bf16[512,512]{1,0:T(8,128)(2,1)S(1)} collective-permute-done((bf16[512,512]{1,0:T(8,128)(2,1)}, bf16[512,512]{1,0:T(8,128)(2,1)S(1)}, u32[]{:S(2)}, u32[]{:S(2)}) %collective-permute-start.22) | collective-permute-done | bytes 524320 | tf_op jit(solution)/shard_map/ppermute | solution.py:413
  150.2 9.4 %collective-permute-start.17 = (bf16[512,512]{1,0:T(8,128)(2,1)}, bf16[512,512]{1,0:T(8,128)(2,1)S(1)}, u32[]{:S(2)}, u32[]{:S(2)}) collective-permute-start(bf16[512,512]{1,0:T(8,128)(2,1)} %get-tuple-element.143), channel_id=1, source_target_pairs={{0,6},{1,7},{2,4},{3,5},{4,2},{5,3},{6,0},{7,1},{8,14},{9,15},{10,... | collective-permute-start | bytes 1572872 | tf_op jit(solution)/shard_map/ppermute | solution.py:413
  159.6 0.7 collective-permute-start.15
  160.3 3.4 %collective-permute-done.21.refs_2_ = bf16[512,512]{1,0:T(8,128)(2,1)S(1)} collective-permute-done((bf16[512,512]{1,0:T(8,128)(2,1)}, bf16[512,512]{1,0:T(8,128)(2,1)S(1)}, u32[]{:S(2)}, u32[]{:S(2)}) %collective-permute-start.21) | collective-permute-done | bytes 524320 | tf_op jit(solution)/shard_map/ppermute | solution.py:413
  163.8 2.2 collective-permute-start.14
  166.0 7.5 %finish.9 = (s32[8,128]{1,0:T(8,128)}, bf16[8192,512]{1,0:T(8,128)(2,1)}) custom-call(s32[16]{0:T(128)S(1)} %broadcast_xor_fusion.place_ref, s32[16]{0:T(128)S(1)} %bitcast.22, f32[8]{0:T(128)S(1)} %broadcast_divide_fusion.factor_ref, bf16[512,512]{1,0:T(8,128)(2,1)} %copy-done.11, ...), custom_call_target="tpu_custom_call", output_to_operand_aliasing={{0}: (9, {}), {1}: (10, {})} | custom-call | tf_op jit(solution)/shard_map/finish/pallas_call | solution.py:359
  173.4 10.3 %finish.10 = (s32[8,128]{1,0:T(8,128)}, bf16[8192,512]{1,0:T(8,128)(2,1)}) custom-call(s32[16]{0:T(128)S(1)} %broadcast_xor_fusion.place_ref, s32[16]{0:T(128)S(1)} %bitcast.23, f32[8]{0:T(128)S(1)} %broadcast_divide_fusion.factor_ref, bf16[512,512]{1,0:T(8,128)(2,1)} %copy-done.10, ...), custom_call_target="tpu_custom_call", output_to_operand_aliasing={{0}: (10, {}), {1}: (11, {})} | custom-call | tf_op jit(solution)/shard_map/finish/pallas_call | solution.py:359
  183.8 8.7 %collective-permute-done.18.refs_2_ = bf16[512,512]{1,0:T(8,128)(2,1)S(1)} collective-permute-done((bf16[512,512]{1,0:T(8,128)(2,1)}, bf16[512,512]{1,0:T(8,128)(2,1)S(1)}, u32[]{:S(2)}, u32[]{:S(2)}) %collective-permute-start.18) | collective-permute-done | bytes 524320 | tf_op jit(solution)/shard_map/ppermute | solution.py:413
  192.5 0.8 copy-done.17
  193.2 10.1 %finish.11 = (s32[8,128]{1,0:T(8,128)}, bf16[8192,512]{1,0:T(8,128)(2,1)}) custom-call(s32[16]{0:T(128)S(1)} %broadcast_xor_fusion.place_ref, s32[16]{0:T(128)S(1)} %bitcast.24, f32[8]{0:T(128)S(1)} %broadcast_divide_fusion.factor_ref, bf16[512,512]{1,0:T(8,128)(2,1)} %copy-done.15, ...), custom_call_target="tpu_custom_call", output_to_operand_aliasing={{0}: (10, {}), {1}: (11, {})} | custom-call | tf_op jit(solution)/shard_map/finish/pallas_call | solution.py:359
  203.4 8.5 %collective-permute-done.15.refs_0_ = bf16[512,512]{1,0:T(8,128)(2,1)S(1)} collective-permute-done((bf16[512,512]{1,0:T(8,128)(2,1)S(1)}, bf16[512,512]{1,0:T(8,128)(2,1)S(1)}, u32[]{:S(2)}, u32[]{:S(2)}) %collective-permute-start.15) | collective-permute-done | bytes 524320 | tf_op jit(solution)/shard_map/ppermute | solution.py:413
  211.9 0.8 copy-done.19
  212.7 4.8 %finish.12 = (s32[8,128]{1,0:T(8,128)}, bf16[8192,512]{1,0:T(8,128)(2,1)}) custom-call(s32[16]{0:T(128)S(1)} %broadcast_xor_fusion.place_ref, s32[16]{0:T(128)S(1)} %bitcast.25, f32[8]{0:T(128)S(1)} %broadcast_divide_fusion.factor_ref, bf16[512,512]{1,0:T(8,128)(2,1)} %copy-done.19, ...), custom_call_target="tpu_custom_call", output_to_operand_aliasing={{0}: (8, {}), {1}: (9, {})} | custom-call | tf_op jit(solution)/shard_map/finish/pallas_call | solution.py:359
  217.5 6.1 %collective-permute-done.14.refs_0_ = bf16[512,512]{1,0:T(8,128)(2,1)S(1)} collective-permute-done((bf16[512,512]{1,0:T(8,128)(2,1)}, bf16[512,512]{1,0:T(8,128)(2,1)S(1)}, u32[]{:S(2)}, u32[]{:S(2)}) %collective-permute-start.14) | collective-permute-done | bytes 524320 | tf_op jit(solution)/shard_map/ppermute | solution.py:413
  223.5 0.8 copy-done.18
  224.4 4.8 %finish.13 = (s32[8,128]{1,0:T(8,128)}, bf16[8192,512]{1,0:T(8,128)(2,1)}) custom-call(s32[16]{0:T(128)S(1)} %broadcast_xor_fusion.place_ref, s32[16]{0:T(128)S(1)} %bitcast.26, f32[8]{0:T(128)S(1)} %broadcast_divide_fusion.factor_ref, bf16[512,512]{1,0:T(8,128)(2,1)} %copy-done.18, ...), custom_call_target="tpu_custom_call", output_to_operand_aliasing={{0}: (8, {}), {1}: (9, {})} | custom-call | tf_op jit(solution)/shard_map/finish/pallas_call | solution.py:359
  (79 shorter events, 4.9 us)
Async XLA Ops:
  0.7 0.8 copy-start.1
  1.4 0.7 copy-start.3
  2.1 8.1 %copy-start.2 = (s32[64,128]{1,0:T(8,128)S(1)}, s32[64,128]{1,0:T(8,128)}, u32[]{:S(2)}) copy-start(s32[64,128]{1,0:T(8,128)} %refs_1_.5) | copy-start | bytes 98308
  2.1 13.7 %copy-start.22 = (f32[8]{0:T(128)S(1)}, f32[8]{0:T(128)}, u32[]{:S(2)}) copy-start(f32[8]{0:T(128)} %param.14) | copy-start | bytes 100
  2.1 13.7 %copy-start.20 = (bf16[8,64,256]{2,1,0:T(8,128)(2,1)S(1)}, bf16[8,64,256]{2,1,0:T(8,128)(2,1)}, u32[]{:S(2)}) copy-start(bf16[8,64,256]{2,1,0:T(8,128)(2,1)} %param.16) | copy-start | bytes 786436
  2.1 14.1 %copy-start.8 = (bf16[512,1024]{1,0:T(8,128)(2,1)S(1)}, bf16[512,1024]{1,0:T(8,128)(2,1)}, u32[]{:S(2)}) copy-start(bf16[512,1024]{1,0:T(8,128)(2,1)} %param.15) | copy-start | bytes 3145732
  6.8 44.9 %collective-permute-start = (bf16[512,512]{1,0:T(8,128)(2,1)}, bf16[512,512]{1,0:T(8,128)(2,1)S(1)}, u32[]{:S(2)}, u32[]{:S(2)}) collective-permute-start(bf16[512,512]{1,0:T(8,128)(2,1)} %get-tuple-element.89), channel_id=1, source_target_pairs={{0,8},{1,9},{2,10},{3,11},{4,12},{5,13},{6,14},{7,15},{8,0},{9,1},... | collective-permute-start | bytes 1572872 | tf_op jit(solution)/shard_map/ppermute | solution.py:413
  14.3 51.5 %collective-permute-start.4 = (bf16[512,512]{1,0:T(8,128)(2,1)}, bf16[512,512]{1,0:T(8,128)(2,1)}, u32[]{:S(2)}, u32[]{:S(2)}) collective-permute-start(bf16[512,512]{1,0:T(8,128)(2,1)} %get-tuple-element.95), channel_id=1, source_target_pairs={{0,9},{1,8},{2,11},{3,10},{4,13},{5,12},{6,15},{7,14},{8,1},{9,0},... | collective-permute-start | bytes 1572872 | tf_op jit(solution)/shard_map/ppermute | solution.py:413
  48.0 40.2 %collective-permute-start.8 = (bf16[512,512]{1,0:T(8,128)(2,1)}, bf16[512,512]{1,0:T(8,128)(2,1)S(1)}, u32[]{:S(2)}, u32[]{:S(2)}) collective-permute-start(bf16[512,512]{1,0:T(8,128)(2,1)} %get-tuple-element.109), channel_id=1, source_target_pairs={{0,10},{1,11},{2,8},{3,9},{4,14},{5,15},{6,12},{7,13},{8,2},{9,3},... | collective-permute-start | bytes 1572872 | tf_op jit(solution)/shard_map/ppermute | solution.py:413
  51.6 0.8 copy-start.5
  52.4 36.6 %copy-start.23 = (s32[16]{0:T(128)S(1)}, s32[16]{0:T(128)}, u32[]{:S(2)}) copy-start(s32[16]{0:T(128)} %constant.30.clone) | copy-start | bytes 196
  52.4 36.7 %copy-start.21 = (bf16[64,192]{1,0:T(8,128)(2,1)S(1)}, bf16[64,192]{1,0:T(8,128)(2,1)}, u32[]{:S(2)}) copy-start(bf16[64,192]{1,0:T(8,128)(2,1)} %param.17) | copy-start | bytes 73732
  53.9 11.9 %collective-permute-start.1 = (bf16[2,80,256]{2,1,0:T(8,128)(2,1)S(1)}, bf16[2,80,256]{2,1,0:T(8,128)(2,1)S(1)}, u32[]{:S(2)}, u32[]{:S(2)}) collective-permute-start(bf16[2,80,256]{2,1,0:T(8,128)(2,1)S(1)} %get-tuple-element.91), channel_id=1, source_target_pairs={{0,1},{1,0},{2,3},{3,2},{4,5},{5,4},{6,7},{7,6},{8,9},{9,8},{10,11... | collective-permute-start | bytes 245768 | tf_op jit(solution)/shard_map/ppermute | solution.py:413
  58.7 8.1 %collective-permute-start.2 = (bf16[2,80,256]{2,1,0:T(8,128)(2,1)S(1)}, bf16[2,80,256]{2,1,0:T(8,128)(2,1)S(1)}, u32[]{:S(2)}, u32[]{:S(2)}) collective-permute-start(bf16[2,80,256]{2,1,0:T(8,128)(2,1)S(1)} %get-tuple-element.92), channel_id=1, source_target_pairs={{0,2},{1,3},{2,0},{3,1},{4,6},{5,7},{6,4},{7,5},{8,10},{9,11},{10,... | collective-permute-start | bytes 245768 | tf_op jit(solution)/shard_map/ppermute | solution.py:413
  58.7 8.1 %collective-permute-start.3 = (bf16[2,80,256]{2,1,0:T(8,128)(2,1)S(1)}, bf16[2,80,256]{2,1,0:T(8,128)(2,1)S(1)}, u32[]{:S(2)}, u32[]{:S(2)}) collective-permute-start(bf16[2,80,256]{2,1,0:T(8,128)(2,1)S(1)} %get-tuple-element.93), channel_id=1, source_target_pairs={{0,3},{1,2},{2,1},{3,0},{4,7},{5,6},{6,5},{7,4},{8,11},{9,10},{10,... | collective-permute-start | bytes 245768 | tf_op jit(solution)/shard_map/ppermute | solution.py:413
  66.8 40.4 %copy-start = (bf16[512,512]{1,0:T(8,128)(2,1)S(1)}, bf16[512,512]{1,0:T(8,128)(2,1)}, u32[]{:S(2)}) copy-start(bf16[512,512]{1,0:T(8,128)(2,1)} %refs_4_.3) | copy-start | bytes 1572868
  81.2 36.2 %collective-permute-start.9 = (bf16[512,512]{1,0:T(8,128)(2,1)}, bf16[512,512]{1,0:T(8,128)(2,1)S(1)}, u32[]{:S(2)}, u32[]{:S(2)}) collective-permute-start(bf16[512,512]{1,0:T(8,128)(2,1)} %get-tuple-element.112), channel_id=1, source_target_pairs={{0,1},{1,0},{2,3},{3,2},{4,5},{5,4},{6,7},{7,6},{8,9},{9,8},{10,11... | collective-permute-start | bytes 1572872 | tf_op jit(solution)/shard_map/ppermute | solution.py:413
  82.0 35.5 %collective-permute-start.10 = (bf16[512,512]{1,0:T(8,128)(2,1)}, bf16[512,512]{1,0:T(8,128)(2,1)}, u32[]{:S(2)}, u32[]{:S(2)}) collective-permute-start(bf16[512,512]{1,0:T(8,128)(2,1)} %get-tuple-element.113), channel_id=1, source_target_pairs={{0,2},{1,3},{2,0},{3,1},{4,6},{5,7},{6,4},{7,5},{8,10},{9,11},{10,... | collective-permute-start | bytes 1572872 | tf_op jit(solution)/shard_map/ppermute | solution.py:413
  83.4 6.3 %collective-permute-start.7 = (bf16[2,80,256]{2,1,0:T(8,128)(2,1)S(1)}, bf16[2,80,256]{2,1,0:T(8,128)(2,1)S(1)}, u32[]{:S(2)}, u32[]{:S(2)}) collective-permute-start(bf16[2,80,256]{2,1,0:T(8,128)(2,1)S(1)} %get-tuple-element.96.refs_1_), channel_id=1, source_target_pairs={{0,12},{1,13},{2,14},{3,15},{4,8},{5,9},{6,10},{7,11},{8,4},{9,5},... | collective-permute-start | bytes 245768 | tf_op jit(solution)/shard_map/ppermute | solution.py:413
  84.9 7.4 %collective-permute-start.6 = (bf16[2,80,256]{2,1,0:T(8,128)(2,1)S(1)}, bf16[2,80,256]{2,1,0:T(8,128)(2,1)S(1)}, u32[]{:S(2)}, u32[]{:S(2)}) collective-permute-start(bf16[2,80,256]{2,1,0:T(8,128)(2,1)S(1)} %get-tuple-element.96.refs_1_), channel_id=1, source_target_pairs={{0,8},{1,9},{2,10},{3,11},{4,12},{5,13},{6,14},{7,15},{8,0},{9,1},... | collective-permute-start | bytes 245768 | tf_op jit(solution)/shard_map/ppermute | solution.py:413
  88.2 0.9 copy-start.6
  88.2 5.3 %collective-permute-start.5 = (bf16[2,80,256]{2,1,0:T(8,128)(2,1)S(1)}, bf16[2,80,256]{2,1,0:T(8,128)(2,1)S(1)}, u32[]{:S(2)}, u32[]{:S(2)}) collective-permute-start(bf16[2,80,256]{2,1,0:T(8,128)(2,1)S(1)} %get-tuple-element.96.refs_1_), channel_id=1, source_target_pairs={{0,4},{1,5},{2,6},{3,7},{4,0},{5,1},{6,2},{7,3},{8,12},{9,13},{10,... | collective-permute-start | bytes 245768 | tf_op jit(solution)/shard_map/ppermute | solution.py:413
  95.8 5.3 %collective-permute-start.13 = (bf16[2,64,256]{2,1,0:T(8,128)(2,1)S(1)}, bf16[2,64,256]{2,1,0:T(8,128)(2,1)S(1)}, u32[]{:S(2)}, u32[]{:S(2)}) collective-permute-start(bf16[2,64,256]{2,1,0:T(8,128)(2,1)S(1)} %get-tuple-element.114.refs_0_), channel_id=1, source_target_pairs={{0,3},{1,2},{2,1},{3,0},{4,7},{5,6},{6,5},{7,4},{8,11},{9,10},{10,... | collective-permute-start | bytes 196616 | tf_op jit(solution)/shard_map/ppermute | solution.py:413
  97.3 4.5 %collective-permute-start.12 = (bf16[2,64,256]{2,1,0:T(8,128)(2,1)S(1)}, bf16[2,64,256]{2,1,0:T(8,128)(2,1)S(1)}, u32[]{:S(2)}, u32[]{:S(2)}) collective-permute-start(bf16[2,64,256]{2,1,0:T(8,128)(2,1)S(1)} %get-tuple-element.114.refs_0_), channel_id=1, source_target_pairs={{0,2},{1,3},{2,0},{3,1},{4,6},{5,7},{6,4},{7,5},{8,10},{9,11},{10,... | collective-permute-start | bytes 196616 | tf_op jit(solution)/shard_map/ppermute | solution.py:413
  98.7 7.2 %collective-permute-start.11 = (bf16[2,64,256]{2,1,0:T(8,128)(2,1)S(1)}, bf16[2,64,256]{2,1,0:T(8,128)(2,1)S(1)}, u32[]{:S(2)}, u32[]{:S(2)}) collective-permute-start(bf16[2,64,256]{2,1,0:T(8,128)(2,1)S(1)} %get-tuple-element.114.refs_0_), channel_id=1, source_target_pairs={{0,1},{1,0},{2,3},{3,2},{4,5},{5,4},{6,7},{7,6},{8,9},{9,8},{10,11... | collective-permute-start | bytes 196616 | tf_op jit(solution)/shard_map/ppermute | solution.py:413
  101.1 36.5 %collective-permute-start.19 = (bf16[512,512]{1,0:T(8,128)(2,1)}, bf16[512,512]{1,0:T(8,128)(2,1)S(1)}, u32[]{:S(2)}, u32[]{:S(2)}) collective-permute-start(bf16[512,512]{1,0:T(8,128)(2,1)} %get-tuple-element.145), channel_id=1, source_target_pairs={{0,12},{1,13},{2,14},{3,15},{4,8},{5,9},{6,10},{7,11},{8,4},{9,5},... | collective-permute-start | bytes 1572872 | tf_op jit(solution)/shard_map/ppermute | solution.py:413
  101.8 48.4 %collective-permute-start.22 = (bf16[512,512]{1,0:T(8,128)(2,1)}, bf16[512,512]{1,0:T(8,128)(2,1)S(1)}, u32[]{:S(2)}, u32[]{:S(2)}) collective-permute-start(bf16[512,512]{1,0:T(8,128)(2,1)} %get-tuple-element.148), channel_id=1, source_target_pairs={{0,11},{1,10},{2,9},{3,8},{4,15},{5,14},{6,13},{7,12},{8,3},{9,2},... | collective-permute-start | bytes 1572872 | tf_op jit(solution)/shard_map/ppermute | solution.py:413
  105.9 53.7 %collective-permute-start.23 = (bf16[512,512]{1,0:T(8,128)(2,1)}, bf16[512,512]{1,0:T(8,128)(2,1)S(1)}, u32[]{:S(2)}, u32[]{:S(2)}) collective-permute-start(bf16[512,512]{1,0:T(8,128)(2,1)} %get-tuple-element.149), channel_id=1, source_target_pairs={{0,3},{1,2},{2,1},{3,0},{4,7},{5,6},{6,5},{7,4},{8,11},{9,10},{10,... | collective-permute-start | bytes 1572872 | tf_op jit(solution)/shard_map/ppermute | solution.py:413
  107.2 30.3 %copy-start.7 = (bf16[512,512]{1,0:T(8,128)(2,1)S(1)}, bf16[512,512]{1,0:T(8,128)(2,1)}, u32[]{:S(2)}) copy-start(bf16[512,512]{1,0:T(8,128)(2,1)} %get-tuple-element.142) | copy-start | bytes 1572868
  117.4 42.3 %copy-start.4 = (bf16[512,512]{1,0:T(8,128)(2,1)S(1)}, bf16[512,512]{1,0:T(8,128)(2,1)}, u32[]{:S(2)}) copy-start(bf16[512,512]{1,0:T(8,128)(2,1)} %get-tuple-element.141) | copy-start | bytes 1572868
  117.4 2.9 %copy-start.9 = (bf16[512,512]{1,0:T(8,128)(2,1)}, bf16[512,512]{1,0:T(8,128)(2,1)S(1)}, u32[]{:S(2)}) copy-start(bf16[512,512]{1,0:T(8,128)(2,1)S(1)} %collective-permute-done.9.refs_1_) | copy-start | bytes 1572868
  117.4 42.2 %collective-permute-start.20 = (bf16[512,512]{1,0:T(8,128)(2,1)}, bf16[512,512]{1,0:T(8,128)(2,1)S(1)}, u32[]{:S(2)}, u32[]{:S(2)}) collective-permute-start(bf16[512,512]{1,0:T(8,128)(2,1)} %get-tuple-element.146), channel_id=1, source_target_pairs={{0,4},{1,5},{2,6},{3,7},{4,0},{5,1},{6,2},{7,3},{8,12},{9,13},{10,... | collective-permute-start | bytes 1572872 | tf_op jit(solution)/shard_map/ppermute | solution.py:413
  117.5 46.3 %collective-permute-start.21 = (bf16[512,512]{1,0:T(8,128)(2,1)}, bf16[512,512]{1,0:T(8,128)(2,1)S(1)}, u32[]{:S(2)}, u32[]{:S(2)}) collective-permute-start(bf16[512,512]{1,0:T(8,128)(2,1)} %get-tuple-element.147), channel_id=1, source_target_pairs={{0,5},{1,4},{2,7},{3,6},{4,1},{5,0},{6,3},{7,2},{8,13},{9,12},{10,... | collective-permute-start | bytes 1572872 | tf_op jit(solution)/shard_map/ppermute | solution.py:413
  137.6 35.9 %copy-start.10 = (bf16[512,512]{1,0:T(8,128)(2,1)}, bf16[512,512]{1,0:T(8,128)(2,1)S(1)}, u32[]{:S(2)}) copy-start(bf16[512,512]{1,0:T(8,128)(2,1)S(1)} %collective-permute-done.19.refs_0_) | copy-start | bytes 1572868
  137.6 46.2 %collective-permute-start.16 = (bf16[512,512]{1,0:T(8,128)(2,1)S(1)}, bf16[512,512]{1,0:T(8,128)(2,1)S(1)}, u32[]{:S(2)}, u32[]{:S(2)}) collective-permute-start(bf16[512,512]{1,0:T(8,128)(2,1)S(1)} %copy-done.7), channel_id=1, source_target_pairs={{0,13},{1,12},{2,15},{3,14},{4,9},{5,8},{6,11},{7,10},{8,5},{9,4},... | collective-permute-start | bytes 1572872 | tf_op jit(solution)/shard_map/ppermute | solution.py:413
  150.2 15.8 %copy-start.11 = (bf16[512,512]{1,0:T(8,128)(2,1)}, bf16[512,512]{1,0:T(8,128)(2,1)S(1)}, u32[]{:S(2)}) copy-start(bf16[512,512]{1,0:T(8,128)(2,1)S(1)} %collective-permute-done.22.refs_0_) | copy-start | bytes 1572868
  150.2 33.6 %collective-permute-start.17 = (bf16[512,512]{1,0:T(8,128)(2,1)}, bf16[512,512]{1,0:T(8,128)(2,1)S(1)}, u32[]{:S(2)}, u32[]{:S(2)}) collective-permute-start(bf16[512,512]{1,0:T(8,128)(2,1)} %get-tuple-element.143), channel_id=1, source_target_pairs={{0,6},{1,7},{2,4},{3,5},{4,2},{5,3},{6,0},{7,1},{8,14},{9,15},{10,... | collective-permute-start | bytes 1572872 | tf_op jit(solution)/shard_map/ppermute | solution.py:413
  159.6 6.3 %copy-start.12 = (bf16[512,512]{1,0:T(8,128)(2,1)}, bf16[512,512]{1,0:T(8,128)(2,1)S(1)}, u32[]{:S(2)}) copy-start(bf16[512,512]{1,0:T(8,128)(2,1)S(1)} %collective-permute-done.23.refs_1_) | copy-start | bytes 1572868
  159.6 32.9 %collective-permute-start.18 = (bf16[512,512]{1,0:T(8,128)(2,1)}, bf16[512,512]{1,0:T(8,128)(2,1)S(1)}, u32[]{:S(2)}, u32[]{:S(2)}) collective-permute-start(bf16[512,512]{1,0:T(8,128)(2,1)} %get-tuple-element.144), channel_id=1, source_target_pairs={{0,7},{1,6},{2,5},{3,4},{4,3},{5,2},{6,1},{7,0},{8,15},{9,14},{10,... | collective-permute-start | bytes 1572872 | tf_op jit(solution)/shard_map/ppermute | solution.py:413
  159.6 13.8 %copy-start.13 = (bf16[512,512]{1,0:T(8,128)(2,1)}, bf16[512,512]{1,0:T(8,128)(2,1)S(1)}, u32[]{:S(2)}) copy-start(bf16[512,512]{1,0:T(8,128)(2,1)S(1)} %collective-permute-done.20.refs_1_) | copy-start | bytes 1572868
  159.6 52.2 %collective-permute-start.15 = (bf16[512,512]{1,0:T(8,128)(2,1)S(1)}, bf16[512,512]{1,0:T(8,128)(2,1)S(1)}, u32[]{:S(2)}, u32[]{:S(2)}) collective-permute-start(bf16[512,512]{1,0:T(8,128)(2,1)S(1)} %copy-done.4), channel_id=1, source_target_pairs={{0,14},{1,15},{2,12},{3,13},{4,10},{5,11},{6,8},{7,9},{8,6},{9,7},... | collective-permute-start | bytes 1572872 | tf_op jit(solution)/shard_map/ppermute | solution.py:413
  163.8 9.7 %copy-start.14 = (bf16[512,512]{1,0:T(8,128)(2,1)}, bf16[512,512]{1,0:T(8,128)(2,1)S(1)}, u32[]{:S(2)}) copy-start(bf16[512,512]{1,0:T(8,128)(2,1)S(1)} %collective-permute-done.21.refs_2_) | copy-start | bytes 1572868
  163.8 59.8 %collective-permute-start.14 = (bf16[512,512]{1,0:T(8,128)(2,1)}, bf16[512,512]{1,0:T(8,128)(2,1)S(1)}, u32[]{:S(2)}, u32[]{:S(2)}) collective-permute-start(bf16[512,512]{1,0:T(8,128)(2,1)} %get-tuple-element.140), channel_id=1, source_target_pairs={{0,15},{1,14},{2,13},{3,12},{4,11},{5,10},{6,9},{7,8},{8,7},{9,6},... | collective-permute-start | bytes 1572872 | tf_op jit(solution)/shard_map/ppermute | solution.py:413
  183.8 8.7 %copy-start.15 = (bf16[512,512]{1,0:T(8,128)(2,1)}, bf16[512,512]{1,0:T(8,128)(2,1)S(1)}, u32[]{:S(2)}) copy-start(bf16[512,512]{1,0:T(8,128)(2,1)S(1)} %collective-permute-done.16.refs_0_) | copy-start | bytes 1572868
  183.8 8.7 %copy-start.16 = (bf16[512,512]{1,0:T(8,128)(2,1)}, bf16[512,512]{1,0:T(8,128)(2,1)S(1)}, u32[]{:S(2)}) copy-start(bf16[512,512]{1,0:T(8,128)(2,1)S(1)} %collective-permute-done.17.refs_1_) | copy-start | bytes 1572868
  192.5 0.8 copy-start.17
  211.9 0.8 copy-start.19
  223.5 0.8 copy-start.18
where the time goes:
time: 230 us; the launch traced here: 229 us
  Pallas kernels  116 us (50%)
  waiting for transfers between devices  57.3 us (25%)
  starting transfers between devices  47.5 us (21%)
  local copies, waits for them, and re-layouts  7.15 us (3%)
    pallas_call x7, Pallas kernels, finish(): pl.pallas_call(functools.partial(finish_kernel, ids, block_rows, len(kept...  57.8 us
    ppermute x24, waiting for transfers between devices, send(): return lax.ppermute(chunk, 'pts', [(i, i ^ k) for i in range(shards)])  57.3 us
    ppermute x24, starting transfers between devices, send(): return lax.ppermute(chunk, 'pts', [(i, i ^ k) for i in range(shards)])  47.5 us
    pallas_call x2, Pallas kernels, summarize(): pl.pallas_call(functools.partial(summary_kernel, pieces, steps[0], 2 * le...  32.8 us
    pallas_call x3, Pallas kernels, gather_blocks(): pl.pallas_call(functools.partial(gather_kernel, plan, offsets, per_peer,...  23.2 us
    unnamed x52, local copies, waits for them, and re-layouts  6.34 us
  transfers between devices with their start and end apart: 24, of which 12 were waited for; matrix products, arithmetic and copies ran while one was open for 1% of the time, Pallas kernels for 47%

commit v1 on v0

--- a/solution.py
+++ b/solution.py
@@ -414,9 +414,10 @@
 
     far = list(range(shards // 2, shards))
     near = list(range(1, shards // 2))
-    first, second = far[:1], far[1:3]
+    near = near[:2] + near[:2:-1] + near[2:3]
+    first, second = far[:1], far[1:3] + near[:2]
     late = [far[6 + i : 7 + i] + near[3 + 2 * i : 5 + 2 * i] for i in range(len(far) - 6)]
-    third = near[:2] + far[3:5] + far[5:6] + near[2:3] + [k for wave in late for k in wave] + [0]
+    third = far[3:5] + far[5:6] + near[2:3] + [k for wave in late for k in wave] + [0]
     ranks = first + second + third
     groups = [[0] + far[:2], far[2:3] + near[:2], far[3:4] + near[2:3]]
     groups += [far[4 + i : 5 + i] + near[3 + 2 * i : 5 + 2 * i] for i in range(len(far) - 4)]
@@ -456,7 +457,7 @@
     held.update(zip(first, chunks))
     depart(first)
     order = gather(second, jnp.zeros((8, 128), jnp.int32))
-    depart(second[:1])
+    depart(far[1:2] + near[:2])
 
     seat = (here % inner)[None]
     rows = -(-shards * shards // slices)
@@ -470,11 +471,11 @@
     (begun,), carried = summarize(
         seat, live_rows, factors, nothing, *weights, (0, steps - 1, steps), 0, carry(order)
     )
-    order = release(carried, second[1:2])
+    order = release(carried, far[2:3])
     pieces, carried = summarize(
-        seat, live_rows, factors, begun, *weights, (steps - 1, steps, steps), inner, carry(order, far[0])
-    )
-    order = release(carried, [], far[0])
+        seat, live_rows, factors, begun, *weights, (steps - 1, steps, steps), inner, carry(order, far[0], *near[:2])
+    )
+    order = release(carried, [], far[0], *near[:2])
     parts = [pieces[0]] + [send(pieces[k], k) for k in range(1, inner)]
     piece = jax.ShapeDtypeStruct(parts[0].shape, jnp.bfloat16)
     (part,), carried = small_call(
@@ -484,7 +485,6 @@
     parts = [part] + [send(part, k * inner) for k in range(1, outer)]
     order = gather(third, order)
     arrived[0] = held.pop(0)
-    depart(third[:2])
     mixed = jax.ShapeDtypeStruct((heads // inner, width, slices), jnp.bfloat16)
     (mixed, tails), carried = small_call(
         attend_kernel,
@@ -494,14 +494,14 @@
         carry(order, far[2]),
         parts=outer,
     )
-    order = release(carried, third[2:4], far[2])
+    order = release(carried, far[3:5], far[2])
     received = tails[1 : 1 + rows].reshape(shards, shards)[:, here].astype(jnp.int32)
     parts = [mixed] + [send(mixed, k) for k in range(1, inner)]
     mixed = jax.ShapeDtypeStruct((heads, width, slices), jnp.bfloat16)
     (mixed,), carried = small_call(
         join_kernel, "join", [seat] + parts, [mixed], carry(order), scalars=1, parts=inner
     )
-    order = release(carried, third[4:6])
+    order = release(carried, far[5:6] + near[2:3])
 
     middle_t = entry_t[channels:]
     sources = here ^ jnp.array(ranks, jnp.int32)

time: 230 us -> 224 us (0.974)
  starting transfers between devices: 47.5 us -> 43.3 us
    ppermute x24, starting transfers between devices: 47.5 us -> 43.3 us  [send(): return lax.ppermute(chunk, 'pts', [(i, i ^ k) for i in range(shards)])]
    unnamed x52 -> x48, local copies, waits for them, and re-layouts: 6.34 us -> 7.05 us
  transfers between devices with their start and end apart: 24 -> 24, of which waited for: 12 -> 9; matrix products, arithmetic and copies ran while one was open for 1% -> 1% of each run, Pallas kernels for 47% -> 47%
where the time goes in v1:
time: 224 us; the launch traced here: 223 us
  Pallas kernels  116 us (52%)
  waiting for transfers between devices  55 us (25%)
  starting transfers between devices  43.3 us (19%)
  local copies, waits for them, and re-layouts  7.87 us (4%)
    pallas_call x7, Pallas kernels, finish(): pl.pallas_call(functools.partial(finish_kernel, ids, block_rows, len(kept...  57.6 us
    ppermute x24, waiting for transfers between devices, send(): return lax.ppermute(chunk, 'pts', [(i, i ^ k) for i in range(shards)])  55 us
    ppermute x24, starting transfers between devices, send(): return lax.ppermute(chunk, 'pts', [(i, i ^ k) for i in range(shards)])  43.3 us
    pallas_call x2, Pallas kernels, summarize(): pl.pallas_call(functools.partial(summary_kernel, pieces, steps[0], 2 * le...  33 us
    pallas_call x3, Pallas kernels, gather_blocks(): pl.pallas_call(functools.partial(gather_kernel, plan, offsets, per_peer,...  23.1 us
    unnamed x48, local copies, waits for them, and re-layouts  7.05 us
  transfers between devices with their start and end apart: 24, of which 9 were waited for; matrix products, arithmetic and copies ran while one was open for 1% of the time, Pallas kernels for 47%

profile of v1, /device:TPU:8, one launch (start us, length us, event | category | flops | bytes accessed | tf_op | source)
XLA Modules:
  0.0 223.5 jit_solution(16950226315046445807)
XLA Ops:
  0.7 0.7 copy-done.1
  1.4 0.7 copy-done.3
  2.1 4.6 %gather_blocks.3 = (s32[64]{0:T(128)S(1)}, s32[16]{0:T(128)S(1)}, bf16[512,512]{1,0:T(8,128)(2,1)}) custom-call(s32[1]{0:T(128)} %bitcast.2.here_ref, s32[1]{0:T(128)S(6)} %copy.123.refs_0_, s32[64]{0:T(128)S(1)} %copy-done.3, s32[64,128]{1,0:T(8,128)S(1)} %copy-done.1, bf16[64,128,512]{2,1,0:T(8,128)(2,1)} %bitcast.27), custom_call_target="tpu_custom_call" | custom-call | tf_op jit(solution)/shard_map/gather_blocks/pallas_call | solution.py:113
  6.7 2.8 %collective-permute-start = (bf16[512,512]{1,0:T(8,128)(2,1)}, bf16[512,512]{1,0:T(8,128)(2,1)S(1)}, u32[]{:S(2)}, u32[]{:S(2)}) collective-permute-start(bf16[512,512]{1,0:T(8,128)(2,1)} %get-tuple-element.91), channel_id=1, source_target_pairs={{0,8},{1,9},{2,10},{3,11},{4,12},{5,13},{6,14},{7,15},{8,0},{9,1},... | collective-permute-start | bytes 1572872 | tf_op jit(solution)/shard_map/ppermute | solution.py:413
  10.1 6.0 %gather_blocks.4 = (s32[8,128]{1,0:T(8,128)}, bf16[512,512]{1,0:T(8,128)(2,1)}, bf16[512,512]{1,0:T(8,128)(2,1)}, bf16[512,512]{1,0:T(8,128)(2,1)}, bf16[512,512]{1,0:T(8,128)(2,1)}) custom-call(s32[1]{0:T(128)} %bitcast.2.here_ref, s32[64]{0:T(128)S(1)} %get-tuple-element.86.refs_0_, s32[64,128]{1,0:T(8,128)S(1)} %copy-done.2, ...), custom_call_target="tpu_custom_call", output_to_operand_aliasing={{0}: (4, {})} | custom-call | tf_op jit(solution)/shard_map/gather_blocks/pallas_call | solution.py:113
  16.1 1.4 collective-permute-start.1
  17.5 1.6 collective-permute-start.2
  19.9 1.5 copy.65
  21.5 31.5 %summarize.2 = (s32[8,128]{1,0:T(8,128)}, bf16[512,512]{1,0:T(8,128)(2,1)}, f32[8,80,256]{2,1,0:T(8,128)S(1)}) custom-call(s32[1]{0:T(128)} %bitcast.1.seat_ref, s32[1]{0:T(128)S(6)} %mul.3.live_ref, f32[8]{0:T(128)S(1)} %broadcast_divide_fusion.factor_ref, f32[8,128]{1,0:T(8,128)S(1)} %broadcast_in_dim.35.before_ref, ...), custom_call_target="tpu_custom_call", output_to_operand_aliasing={{0}: (8, {}), {1}: (9, {})} | custom-call | tf_op jit(solution)/shard_map/summarize/pallas_call | solution.py:203
  53.0 2.6 %collective-permute-start.10 = (bf16[512,512]{1,0:T(8,128)(2,1)}, bf16[512,512]{1,0:T(8,128)(2,1)}, u32[]{:S(2)}, u32[]{:S(2)}) collective-permute-start(bf16[512,512]{1,0:T(8,128)(2,1)} %get-tuple-element.113), channel_id=1, source_target_pairs={{0,10},{1,11},{2,8},{3,9},{4,14},{5,15},{6,12},{7,13},{8,2},{9,3},... | collective-permute-start | bytes 1572872 | tf_op jit(solution)/shard_map/ppermute | solution.py:413
  55.7 0.8 copy-done.5
  56.7 1.5 summarize.3
  58.2 5.7 %collective-permute-start.3 = (bf16[2,80,256]{2,1,0:T(8,128)(2,1)S(1)}, bf16[2,80,256]{2,1,0:T(8,128)(2,1)S(1)}, u32[]{:S(2)}, u32[]{:S(2)}) collective-permute-start(bf16[2,80,256]{2,1,0:T(8,128)(2,1)S(1)} %get-tuple-element.95), channel_id=1, source_target_pairs={{0,1},{1,0},{2,3},{3,2},{4,5},{5,4},{6,7},{7,6},{8,9},{9,8},{10,11... | collective-permute-start | bytes 245768 | tf_op jit(solution)/shard_map/ppermute | solution.py:413
  63.9 1.6 collective-permute-start.4
  66.3 4.9 %collective-permute-done.4.refs_2_ = bf16[2,80,256]{2,1,0:T(8,128)(2,1)S(1)} collective-permute-done((bf16[2,80,256]{2,1,0:T(8,128)(2,1)S(1)}, bf16[2,80,256]{2,1,0:T(8,128)(2,1)S(1)}, u32[]{:S(2)}, u32[]{:S(2)}) %collective-permute-start.4) | collective-permute-done | bytes 81952 | tf_op jit(solution)/shard_map/ppermute | solution.py:413
  71.3 1.5 collective-permute-start.9
  72.8 1.7 collective-permute-start.8
  75.0 12.5 %gather_blocks.5 = (s32[8,128]{1,0:T(8,128)}, bf16[512,512]{1,0:T(8,128)(2,1)}, bf16[512,512]{1,0:T(8,128)(2,1)}, bf16[512,512]{1,0:T(8,128)(2,1)}, bf16[512,512...) custom-call(s32[1]{0:T(128)} %bitcast.2.here_ref, ...), custom_call_target="tpu_custom_call", output_to_operand_aliasing={{0}: (4, {})} | custom-call | tf_op jit(solution)/shard_map/gather_blocks/pallas_call | solution.py:113
  87.6 2.3 %attend.1 = (s32[8,128]{1,0:T(8,128)}, bf16[512,512]{1,0:T(8,128)(2,1)}, bf16[512,512]{1,0:T(8,128)(2,1)}, bf16[512,512]{1,0:T(8,128)(2,1)}, bf16[512,512]{1,0:T...) custom-call(bf16[192,64]{1,0:T(8,128)(2,1)S(1)} %bitcast.19, ...), custom_call_target="tpu_custom_call", output_to_operand_aliasing={{0}: (5, {}), {1}: (6, {}), {2}: (7, {}), {3}: (8, {}), {4}... | custom-call | tf_op jit(solution)/shard_map/attend/pallas_call | solution.py:240
  89.9 1.4 collective-permute-start.13
  91.3 1.5 collective-permute-start.12
  92.8 0.6 collective-permute-start.11
  93.7 1.5 collective-permute-start.19
  95.2 2.1 collective-permute-start.22
  97.4 1.8 collective-permute-start.23
  99.2 10.1 %finish.7 = (s32[8,128]{1,0:T(8,128)}, bf16[512,512]{1,0:T(8,128)(2,1)}, bf16[512,512]{1,0:T(8,128)(2,1)}, bf16[512,512]{1,0:T(8,128)(2,1)}, bf16[512,512]{1,0:T...) custom-call(s32[16]{0:T(128)S(1)} %broadcast_xor_fusion.place_ref, ...), custom_call_target="tpu_custom_call", output_to_operand_aliasing={{0}: (10, {}), {1}: (11, {}), {2}: (12, {}), {3}: (13, {}),... | custom-call | tf_op jit(solution)/shard_map/finish/pallas_call | solution.py:359
  109.3 2.0 collective-permute-start.20
  111.3 0.8 collective-permute-start.21
  112.1 10.1 %finish.8 = (s32[8,128]{1,0:T(8,128)}, bf16[512,512]{1,0:T(8,128)(2,1)}, bf16[512,512]{1,0:T(8,128)(2,1)}, bf16[512,512]{1,0:T(8,128)(2,1)}, bf16[8192,512]{1,0:T(8,128)(2,1)}) custom-call(s32[16]{0:T(128)S(1)} %broadcast_xor_fusion.place_ref, s32[16]{0:T(128)S(1)} %bitcast.21, ...), custom_call_target="tpu_custom_call", output_to_operand_aliasing={{0}: (10, {}), {1}: (11, {}), {2}: (12, {}), {3}: (13, {}),... | custom-call | tf_op jit(solution)/shard_map/finish/pallas_call | solution.py:359
  122.1 7.3 %collective-permute-done.19.refs_0_ = bf16[512,512]{1,0:T(8,128)(2,1)S(1)} collective-permute-done((bf16[512,512]{1,0:T(8,128)(2,1)}, bf16[512,512]{1,0:T(8,128)(2,1)S(1)}, u32[]{:S(2)}, u32[]{:S(2)}) %collective-permute-start.19) | collective-permute-done | bytes 524320 | tf_op jit(solution)/shard_map/ppermute | solution.py:413
  129.4 2.6 %collective-permute-start.16 = (bf16[512,512]{1,0:T(8,128)(2,1)S(1)}, bf16[512,512]{1,0:T(8,128)(2,1)S(1)}, u32[]{:S(2)}, u32[]{:S(2)}) collective-permute-start(bf16[512,512]{1,0:T(8,128)(2,1)S(1)} %copy-done.7), channel_id=1, source_target_pairs={{0,13},{1,12},{2,15},{3,14},{4,9},{5,8},{6,11},{7,10},{8,5},{9,4},... | collective-permute-start | bytes 1572872 | tf_op jit(solution)/shard_map/ppermute | solution.py:413
  131.9 7.9 %collective-permute-done.22.refs_0_ = bf16[512,512]{1,0:T(8,128)(2,1)S(1)} collective-permute-done((bf16[512,512]{1,0:T(8,128)(2,1)}, bf16[512,512]{1,0:T(8,128)(2,1)S(1)}, u32[]{:S(2)}, u32[]{:S(2)}) %collective-permute-start.22) | collective-permute-done | bytes 524320 | tf_op jit(solution)/shard_map/ppermute | solution.py:413
  139.8 3.7 %collective-permute-start.17 = (bf16[512,512]{1,0:T(8,128)(2,1)}, bf16[512,512]{1,0:T(8,128)(2,1)S(1)}, u32[]{:S(2)}, u32[]{:S(2)}) collective-permute-start(bf16[512,512]{1,0:T(8,128)(2,1)} %get-tuple-element.147), channel_id=1, source_target_pairs={{0,4},{1,5},{2,6},{3,7},{4,0},{5,1},{6,2},{7,3},{8,12},{9,13},{10,... | collective-permute-start | bytes 1572872 | tf_op jit(solution)/shard_map/ppermute | solution.py:413
  143.6 1.1 collective-permute-start.18
  144.7 3.4 %collective-permute-start.15 = (bf16[512,512]{1,0:T(8,128)(2,1)S(1)}, bf16[512,512]{1,0:T(8,128)(2,1)S(1)}, u32[]{:S(2)}, u32[]{:S(2)}) collective-permute-start(bf16[512,512]{1,0:T(8,128)(2,1)S(1)} %copy-done.4), channel_id=1, source_target_pairs={{0,14},{1,15},{2,12},{3,13},{4,10},{5,11},{6,8},{7,9},{8,6},{9,7},... | collective-permute-start | bytes 1572872 | tf_op jit(solution)/shard_map/ppermute | solution.py:413
  148.1 14.1 %collective-permute-done.21.refs_2_ = bf16[512,512]{1,0:T(8,128)(2,1)S(1)} collective-permute-done((bf16[512,512]{1,0:T(8,128)(2,1)}, bf16[512,512]{1,0:T(8,128)(2,1)S(1)}, u32[]{:S(2)}, u32[]{:S(2)}) %collective-permute-start.21) | collective-permute-done | bytes 524320 | tf_op jit(solution)/shard_map/ppermute | solution.py:413
  162.1 1.2 collective-permute-start.14
  163.3 7.4 %finish.9 = (s32[8,128]{1,0:T(8,128)}, bf16[8192,512]{1,0:T(8,128)(2,1)}) custom-call(s32[16]{0:T(128)S(1)} %broadcast_xor_fusion.place_ref, s32[16]{0:T(128)S(1)} %bitcast.22, f32[8]{0:T(128)S(1)} %broadcast_divide_fusion.factor_ref, bf16[512,512]{1,0:T(8,128)(2,1)} %copy-done.9, ...), custom_call_target="tpu_custom_call", output_to_operand_aliasing={{0}: (9, {}), {1}: (10, {})} | custom-call | tf_op jit(solution)/shard_map/finish/pallas_call | solution.py:359
  170.8 10.3 %finish.10 = (s32[8,128]{1,0:T(8,128)}, bf16[8192,512]{1,0:T(8,128)(2,1)}) custom-call(s32[16]{0:T(128)S(1)} %broadcast_xor_fusion.place_ref, s32[16]{0:T(128)S(1)} %bitcast.23, f32[8]{0:T(128)S(1)} %broadcast_divide_fusion.factor_ref, bf16[512,512]{1,0:T(8,128)(2,1)} %copy-done.8, ...), custom_call_target="tpu_custom_call", output_to_operand_aliasing={{0}: (10, {}), {1}: (11, {})} | custom-call | tf_op jit(solution)/shard_map/finish/pallas_call | solution.py:359
  181.1 2.5 %collective-permute-done.17.refs_1_ = bf16[512,512]{1,0:T(8,128)(2,1)S(1)} collective-permute-done((bf16[512,512]{1,0:T(8,128)(2,1)}, bf16[512,512]{1,0:T(8,128)(2,1)S(1)}, u32[]{:S(2)}, u32[]{:S(2)}) %collective-permute-start.17) | collective-permute-done | bytes 524320 | tf_op jit(solution)/shard_map/ppermute | solution.py:413
  183.6 0.8 copy-done.14
  184.6 10.1 %finish.11 = (s32[8,128]{1,0:T(8,128)}, bf16[8192,512]{1,0:T(8,128)(2,1)}) custom-call(s32[16]{0:T(128)S(1)} %broadcast_xor_fusion.place_ref, s32[16]{0:T(128)S(1)} %bitcast.24, f32[8]{0:T(128)S(1)} %broadcast_divide_fusion.factor_ref, bf16[512,512]{1,0:T(8,128)(2,1)} %copy-done.13, ...), custom_call_target="tpu_custom_call", output_to_operand_aliasing={{0}: (10, {}), {1}: (11, {})} | custom-call | tf_op jit(solution)/shard_map/finish/pallas_call | solution.py:359
  194.7 10.4 %collective-permute-done.15.refs_0_ = bf16[512,512]{1,0:T(8,128)(2,1)S(1)} collective-permute-done((bf16[512,512]{1,0:T(8,128)(2,1)S(1)}, bf16[512,512]{1,0:T(8,128)(2,1)S(1)}, u32[]{:S(2)}, u32[]{:S(2)}) %collective-permute-start.15) | collective-permute-done | bytes 524320 | tf_op jit(solution)/shard_map/ppermute | solution.py:413
  205.1 0.8 copy-done.17
  205.9 4.8 %finish.12 = (s32[8,128]{1,0:T(8,128)}, bf16[8192,512]{1,0:T(8,128)(2,1)}) custom-call(s32[16]{0:T(128)S(1)} %broadcast_xor_fusion.place_ref, s32[16]{0:T(128)S(1)} %bitcast.25, f32[8]{0:T(128)S(1)} %broadcast_divide_fusion.factor_ref, bf16[512,512]{1,0:T(8,128)(2,1)} %copy-done.17, ...), custom_call_target="tpu_custom_call", output_to_operand_aliasing={{0}: (8, {}), {1}: (9, {})} | custom-call | tf_op jit(solution)/shard_map/finish/pallas_call | solution.py:359
  210.7 7.2 %collective-permute-done.14.refs_0_ = bf16[512,512]{1,0:T(8,128)(2,1)S(1)} collective-permute-done((bf16[512,512]{1,0:T(8,128)(2,1)}, bf16[512,512]{1,0:T(8,128)(2,1)S(1)}, u32[]{:S(2)}, u32[]{:S(2)}) %collective-permute-start.14) | collective-permute-done | bytes 524320 | tf_op jit(solution)/shard_map/ppermute | solution.py:413
  217.9 0.8 copy-done.16
  218.7 4.8 %finish.13 = (s32[8,128]{1,0:T(8,128)}, bf16[8192,512]{1,0:T(8,128)(2,1)}) custom-call(s32[16]{0:T(128)S(1)} %broadcast_xor_fusion.place_ref, s32[16]{0:T(128)S(1)} %bitcast.26, f32[8]{0:T(128)S(1)} %broadcast_divide_fusion.factor_ref, bf16[512,512]{1,0:T(8,128)(2,1)} %copy-done.16, ...), custom_call_target="tpu_custom_call", output_to_operand_aliasing={{0}: (8, {}), {1}: (9, {})} | custom-call | tf_op jit(solution)/shard_map/finish/pallas_call | solution.py:359
  (75 shorter events, 3.5 us)
Async XLA Ops:
  0.7 0.8 copy-start.1
  1.4 0.7 copy-start.3
  2.1 8.0 %copy-start.2 = (s32[64,128]{1,0:T(8,128)S(1)}, s32[64,128]{1,0:T(8,128)}, u32[]{:S(2)}) copy-start(s32[64,128]{1,0:T(8,128)} %refs_1_.5) | copy-start | bytes 98308
  2.1 17.5 %copy-start.18 = (bf16[8,64,256]{2,1,0:T(8,128)(2,1)S(1)}, bf16[8,64,256]{2,1,0:T(8,128)(2,1)}, u32[]{:S(2)}) copy-start(bf16[8,64,256]{2,1,0:T(8,128)(2,1)} %param.16) | copy-start | bytes 786436
  2.1 19.4 %copy-start.20 = (f32[8]{0:T(128)S(1)}, f32[8]{0:T(128)}, u32[]{:S(2)}) copy-start(f32[8]{0:T(128)} %param.14) | copy-start | bytes 100
  6.7 48.9 %collective-permute-start = (bf16[512,512]{1,0:T(8,128)(2,1)}, bf16[512,512]{1,0:T(8,128)(2,1)S(1)}, u32[]{:S(2)}, u32[]{:S(2)}) collective-permute-start(bf16[512,512]{1,0:T(8,128)(2,1)} %get-tuple-element.91), channel_id=1, source_target_pairs={{0,8},{1,9},{2,10},{3,11},{4,12},{5,13},{6,14},{7,15},{8,0},{9,1},... | collective-permute-start | bytes 1572872 | tf_op jit(solution)/shard_map/ppermute | solution.py:413
  16.1 39.6 %collective-permute-start.1 = (bf16[512,512]{1,0:T(8,128)(2,1)}, bf16[512,512]{1,0:T(8,128)(2,1)S(1)}, u32[]{:S(2)}, u32[]{:S(2)}) collective-permute-start(bf16[512,512]{1,0:T(8,128)(2,1)} %get-tuple-element.92), channel_id=1, source_target_pairs={{0,1},{1,0},{2,3},{3,2},{4,5},{5,4},{6,7},{7,6},{8,9},{9,8},{10,11... | collective-permute-start | bytes 1572872 | tf_op jit(solution)/shard_map/ppermute | solution.py:413
  17.5 38.2 %collective-permute-start.2 = (bf16[512,512]{1,0:T(8,128)(2,1)}, bf16[512,512]{1,0:T(8,128)(2,1)}, u32[]{:S(2)}, u32[]{:S(2)}) collective-permute-start(bf16[512,512]{1,0:T(8,128)(2,1)} %get-tuple-element.93), channel_id=1, source_target_pairs={{0,2},{1,3},{2,0},{3,1},{4,6},{5,7},{6,4},{7,5},{8,10},{9,11},{10,... | collective-permute-start | bytes 1572872 | tf_op jit(solution)/shard_map/ppermute | solution.py:413
  19.1 46.8 %collective-permute-start.6 = (bf16[512,512]{1,0:T(8,128)(2,1)}, bf16[512,512]{1,0:T(8,128)(2,1)}, u32[]{:S(2)}, u32[]{:S(2)}) collective-permute-start(bf16[512,512]{1,0:T(8,128)(2,1)} %get-tuple-element.99), channel_id=1, source_target_pairs={{0,9},{1,8},{2,11},{3,10},{4,13},{5,12},{6,15},{7,14},{8,1},{9,0},... | collective-permute-start | bytes 1572872 | tf_op jit(solution)/shard_map/ppermute | solution.py:413
  53.0 21.9 %copy-start.21 = (s32[16]{0:T(128)S(1)}, s32[16]{0:T(128)}, u32[]{:S(2)}) copy-start(s32[16]{0:T(128)} %constant.30.clone) | copy-start | bytes 196
  53.0 21.9 %copy-start.19 = (bf16[64,192]{1,0:T(8,128)(2,1)S(1)}, bf16[64,192]{1,0:T(8,128)(2,1)}, u32[]{:S(2)}) copy-start(bf16[64,192]{1,0:T(8,128)(2,1)} %param.17) | copy-start | bytes 73732
  53.0 34.5 %collective-permute-start.10 = (bf16[512,512]{1,0:T(8,128)(2,1)}, bf16[512,512]{1,0:T(8,128)(2,1)}, u32[]{:S(2)}, u32[]{:S(2)}) collective-permute-start(bf16[512,512]{1,0:T(8,128)(2,1)} %get-tuple-element.113), channel_id=1, source_target_pairs={{0,10},{1,11},{2,8},{3,9},{4,14},{5,15},{6,12},{7,13},{8,2},{9,3},... | collective-permute-start | bytes 1572872 | tf_op jit(solution)/shard_map/ppermute | solution.py:413
  55.7 0.9 copy-start.5
  55.7 1.1 copy-start.6
  58.2 8.1 %collective-permute-start.3 = (bf16[2,80,256]{2,1,0:T(8,128)(2,1)S(1)}, bf16[2,80,256]{2,1,0:T(8,128)(2,1)S(1)}, u32[]{:S(2)}, u32[]{:S(2)}) collective-permute-start(bf16[2,80,256]{2,1,0:T(8,128)(2,1)S(1)} %get-tuple-element.95), channel_id=1, source_target_pairs={{0,1},{1,0},{2,3},{3,2},{4,5},{5,4},{6,7},{7,6},{8,9},{9,8},{10,11... | collective-permute-start | bytes 245768 | tf_op jit(solution)/shard_map/ppermute | solution.py:413
  63.9 7.3 %collective-permute-start.4 = (bf16[2,80,256]{2,1,0:T(8,128)(2,1)S(1)}, bf16[2,80,256]{2,1,0:T(8,128)(2,1)S(1)}, u32[]{:S(2)}, u32[]{:S(2)}) collective-permute-start(bf16[2,80,256]{2,1,0:T(8,128)(2,1)S(1)} %get-tuple-element.96), channel_id=1, source_target_pairs={{0,2},{1,3},{2,0},{3,1},{4,6},{5,7},{6,4},{7,5},{8,10},{9,11},{10,... | collective-permute-start | bytes 245768 | tf_op jit(solution)/shard_map/ppermute | solution.py:413
  65.5 5.7 %collective-permute-start.5 = (bf16[2,80,256]{2,1,0:T(8,128)(2,1)S(1)}, bf16[2,80,256]{2,1,0:T(8,128)(2,1)S(1)}, u32[]{:S(2)}, u32[]{:S(2)}) collective-permute-start(bf16[2,80,256]{2,1,0:T(8,128)(2,1)S(1)} %get-tuple-element.97), channel_id=1, source_target_pairs={{0,3},{1,2},{2,1},{3,0},{4,7},{5,6},{6,5},{7,4},{8,11},{9,10},{10,... | collective-permute-start | bytes 245768 | tf_op jit(solution)/shard_map/ppermute | solution.py:413
  71.3 16.3 %collective-permute-start.9 = (bf16[2,80,256]{2,1,0:T(8,128)(2,1)S(1)}, bf16[2,80,256]{2,1,0:T(8,128)(2,1)S(1)}, u32[]{:S(2)}, u32[]{:S(2)}) collective-permute-start(bf16[2,80,256]{2,1,0:T(8,128)(2,1)S(1)} %get-tuple-element.100.refs_1_), channel_id=1, source_target_pairs={{0,12},{1,13},{2,14},{3,15},{4,8},{5,9},{6,10},{7,11},{8,4},{9,5},... | collective-permute-start | bytes 245768 | tf_op jit(solution)/shard_map/ppermute | solution.py:413
  72.8 14.8 %collective-permute-start.8 = (bf16[2,80,256]{2,1,0:T(8,128)(2,1)S(1)}, bf16[2,80,256]{2,1,0:T(8,128)(2,1)S(1)}, u32[]{:S(2)}, u32[]{:S(2)}) collective-permute-start(bf16[2,80,256]{2,1,0:T(8,128)(2,1)S(1)} %get-tuple-element.100.refs_1_), channel_id=1, source_target_pairs={{0,8},{1,9},{2,10},{3,11},{4,12},{5,13},{6,14},{7,15},{8,0},{9,1},... | collective-permute-start | bytes 245768 | tf_op jit(solution)/shard_map/ppermute | solution.py:413
  74.5 13.1 %collective-permute-start.7 = (bf16[2,80,256]{2,1,0:T(8,128)(2,1)S(1)}, bf16[2,80,256]{2,1,0:T(8,128)(2,1)S(1)}, u32[]{:S(2)}, u32[]{:S(2)}) collective-permute-start(bf16[2,80,256]{2,1,0:T(8,128)(2,1)S(1)} %get-tuple-element.100.refs_1_), channel_id=1, source_target_pairs={{0,4},{1,5},{2,6},{3,7},{4,0},{5,1},{6,2},{7,3},{8,12},{9,13},{10,... | collective-permute-start | bytes 245768 | tf_op jit(solution)/shard_map/ppermute | solution.py:413
  75.0 24.1 %copy-start = (bf16[512,512]{1,0:T(8,128)(2,1)S(1)}, bf16[512,512]{1,0:T(8,128)(2,1)}, u32[]{:S(2)}) copy-start(bf16[512,512]{1,0:T(8,128)(2,1)} %refs_4_.3) | copy-start | bytes 1572868
  89.9 7.4 %collective-permute-start.13 = (bf16[2,64,256]{2,1,0:T(8,128)(2,1)S(1)}, bf16[2,64,256]{2,1,0:T(8,128)(2,1)S(1)}, u32[]{:S(2)}, u32[]{:S(2)}) collective-permute-start(bf16[2,64,256]{2,1,0:T(8,128)(2,1)S(1)} %get-tuple-element.118.refs_0_), channel_id=1, source_target_pairs={{0,3},{1,2},{2,1},{3,0},{4,7},{5,6},{6,5},{7,4},{8,11},{9,10},{10,... | collective-permute-start | bytes 196616 | tf_op jit(solution)/shard_map/ppermute | solution.py:413
  91.3 6.0 %collective-permute-start.12 = (bf16[2,64,256]{2,1,0:T(8,128)(2,1)S(1)}, bf16[2,64,256]{2,1,0:T(8,128)(2,1)S(1)}, u32[]{:S(2)}, u32[]{:S(2)}) collective-permute-start(bf16[2,64,256]{2,1,0:T(8,128)(2,1)S(1)} %get-tuple-element.118.refs_0_), channel_id=1, source_target_pairs={{0,2},{1,3},{2,0},{3,1},{4,6},{5,7},{6,4},{7,5},{8,10},{9,11},{10,... | collective-permute-start | bytes 196616 | tf_op jit(solution)/shard_map/ppermute | solution.py:413
  92.8 4.5 %collective-permute-start.11 = (bf16[2,64,256]{2,1,0:T(8,128)(2,1)S(1)}, bf16[2,64,256]{2,1,0:T(8,128)(2,1)S(1)}, u32[]{:S(2)}, u32[]{:S(2)}) collective-permute-start(bf16[2,64,256]{2,1,0:T(8,128)(2,1)S(1)} %get-tuple-element.118.refs_0_), channel_id=1, source_target_pairs={{0,1},{1,0},{2,3},{3,2},{4,5},{5,4},{6,7},{7,6},{8,9},{9,8},{10,11... | collective-permute-start | bytes 196616 | tf_op jit(solution)/shard_map/ppermute | solution.py:413
  93.7 35.6 %collective-permute-start.19 = (bf16[512,512]{1,0:T(8,128)(2,1)}, bf16[512,512]{1,0:T(8,128)(2,1)S(1)}, u32[]{:S(2)}, u32[]{:S(2)}) collective-permute-start(bf16[512,512]{1,0:T(8,128)(2,1)} %get-tuple-element.149), channel_id=1, source_target_pairs={{0,12},{1,13},{2,14},{3,15},{4,8},{5,9},{6,10},{7,11},{8,4},{9,5},... | collective-permute-start | bytes 1572872 | tf_op jit(solution)/shard_map/ppermute | solution.py:413
  95.2 44.6 %collective-permute-start.22 = (bf16[512,512]{1,0:T(8,128)(2,1)}, bf16[512,512]{1,0:T(8,128)(2,1)S(1)}, u32[]{:S(2)}, u32[]{:S(2)}) collective-permute-start(bf16[512,512]{1,0:T(8,128)(2,1)} %get-tuple-element.152), channel_id=1, source_target_pairs={{0,11},{1,10},{2,9},{3,8},{4,15},{5,14},{6,13},{7,12},{8,3},{9,2},... | collective-permute-start | bytes 1572872 | tf_op jit(solution)/shard_map/ppermute | solution.py:413
  97.4 46.2 %collective-permute-start.23 = (bf16[512,512]{1,0:T(8,128)(2,1)}, bf16[512,512]{1,0:T(8,128)(2,1)S(1)}, u32[]{:S(2)}, u32[]{:S(2)}) collective-permute-start(bf16[512,512]{1,0:T(8,128)(2,1)} %get-tuple-element.153), channel_id=1, source_target_pairs={{0,7},{1,6},{2,5},{3,4},{4,3},{5,2},{6,1},{7,0},{8,15},{9,14},{10,... | collective-permute-start | bytes 1572872 | tf_op jit(solution)/shard_map/ppermute | solution.py:413
  99.2 30.2 %copy-start.7 = (bf16[512,512]{1,0:T(8,128)(2,1)S(1)}, bf16[512,512]{1,0:T(8,128)(2,1)}, u32[]{:S(2)}) copy-start(bf16[512,512]{1,0:T(8,128)(2,1)} %get-tuple-element.146) | copy-start | bytes 1572868
  109.3 35.4 %copy-start.4 = (bf16[512,512]{1,0:T(8,128)(2,1)S(1)}, bf16[512,512]{1,0:T(8,128)(2,1)}, u32[]{:S(2)}) copy-start(bf16[512,512]{1,0:T(8,128)(2,1)} %get-tuple-element.145) | copy-start | bytes 1572868
  109.3 35.4 %collective-permute-start.20 = (bf16[512,512]{1,0:T(8,128)(2,1)}, bf16[512,512]{1,0:T(8,128)(2,1)S(1)}, u32[]{:S(2)}, u32[]{:S(2)}) collective-permute-start(bf16[512,512]{1,0:T(8,128)(2,1)} %get-tuple-element.150), channel_id=1, source_target_pairs={{0,6},{1,7},{2,4},{3,5},{4,2},{5,3},{6,0},{7,1},{8,14},{9,15},{10,... | collective-permute-start | bytes 1572872 | tf_op jit(solution)/shard_map/ppermute | solution.py:413
  111.3 50.8 %collective-permute-start.21 = (bf16[512,512]{1,0:T(8,128)(2,1)}, bf16[512,512]{1,0:T(8,128)(2,1)S(1)}, u32[]{:S(2)}, u32[]{:S(2)}) collective-permute-start(bf16[512,512]{1,0:T(8,128)(2,1)} %get-tuple-element.151), channel_id=1, source_target_pairs={{0,5},{1,4},{2,7},{3,6},{4,1},{5,0},{6,3},{7,2},{8,13},{9,12},{10,... | collective-permute-start | bytes 1572872 | tf_op jit(solution)/shard_map/ppermute | solution.py:413
  129.4 41.4 %copy-start.8 = (bf16[512,512]{1,0:T(8,128)(2,1)}, bf16[512,512]{1,0:T(8,128)(2,1)S(1)}, u32[]{:S(2)}) copy-start(bf16[512,512]{1,0:T(8,128)(2,1)S(1)} %collective-permute-done.19.refs_0_) | copy-start | bytes 1572868
  129.4 51.7 %collective-permute-start.16 = (bf16[512,512]{1,0:T(8,128)(2,1)S(1)}, bf16[512,512]{1,0:T(8,128)(2,1)S(1)}, u32[]{:S(2)}, u32[]{:S(2)}) collective-permute-start(bf16[512,512]{1,0:T(8,128)(2,1)S(1)} %copy-done.7), channel_id=1, source_target_pairs={{0,13},{1,12},{2,15},{3,14},{4,9},{5,8},{6,11},{7,10},{8,5},{9,4},... | collective-permute-start | bytes 1572872 | tf_op jit(solution)/shard_map/ppermute | solution.py:413
  139.8 23.5 %copy-start.9 = (bf16[512,512]{1,0:T(8,128)(2,1)}, bf16[512,512]{1,0:T(8,128)(2,1)S(1)}, u32[]{:S(2)}) copy-start(bf16[512,512]{1,0:T(8,128)(2,1)S(1)} %collective-permute-done.22.refs_0_) | copy-start | bytes 1572868
  139.8 43.7 %collective-permute-start.17 = (bf16[512,512]{1,0:T(8,128)(2,1)}, bf16[512,512]{1,0:T(8,128)(2,1)S(1)}, u32[]{:S(2)}, u32[]{:S(2)}) collective-permute-start(bf16[512,512]{1,0:T(8,128)(2,1)} %get-tuple-element.147), channel_id=1, source_target_pairs={{0,4},{1,5},{2,6},{3,7},{4,0},{5,1},{6,2},{7,3},{8,12},{9,13},{10,... | collective-permute-start | bytes 1572872 | tf_op jit(solution)/shard_map/ppermute | solution.py:413
  143.6 19.8 %copy-start.10 = (bf16[512,512]{1,0:T(8,128)(2,1)}, bf16[512,512]{1,0:T(8,128)(2,1)S(1)}, u32[]{:S(2)}) copy-start(bf16[512,512]{1,0:T(8,128)(2,1)S(1)} %collective-permute-done.23.refs_1_) | copy-start | bytes 1572868
  143.6 40.0 %collective-permute-start.18 = (bf16[512,512]{1,0:T(8,128)(2,1)}, bf16[512,512]{1,0:T(8,128)(2,1)S(1)}, u32[]{:S(2)}, u32[]{:S(2)}) collective-permute-start(bf16[512,512]{1,0:T(8,128)(2,1)} %get-tuple-element.148), channel_id=1, source_target_pairs={{0,3},{1,2},{2,1},{3,0},{4,7},{5,6},{6,5},{7,4},{8,11},{9,10},{10,... | collective-permute-start | bytes 1572872 | tf_op jit(solution)/shard_map/ppermute | solution.py:413
  144.7 26.1 %copy-start.11 = (bf16[512,512]{1,0:T(8,128)(2,1)}, bf16[512,512]{1,0:T(8,128)(2,1)S(1)}, u32[]{:S(2)}) copy-start(bf16[512,512]{1,0:T(8,128)(2,1)S(1)} %collective-permute-done.20.refs_1_) | copy-start | bytes 1572868
  144.7 60.4 %collective-permute-start.15 = (bf16[512,512]{1,0:T(8,128)(2,1)S(1)}, bf16[512,512]{1,0:T(8,128)(2,1)S(1)}, u32[]{:S(2)}, u32[]{:S(2)}) collective-permute-start(bf16[512,512]{1,0:T(8,128)(2,1)S(1)} %copy-done.4), channel_id=1, source_target_pairs={{0,14},{1,15},{2,12},{3,13},{4,10},{5,11},{6,8},{7,9},{8,6},{9,7},... | collective-permute-start | bytes 1572872 | tf_op jit(solution)/shard_map/ppermute | solution.py:413
  162.1 8.7 %copy-start.12 = (bf16[512,512]{1,0:T(8,128)(2,1)}, bf16[512,512]{1,0:T(8,128)(2,1)S(1)}, u32[]{:S(2)}) copy-start(bf16[512,512]{1,0:T(8,128)(2,1)S(1)} %collective-permute-done.21.refs_2_) | copy-start | bytes 1572868
  162.1 55.8 %collective-permute-start.14 = (bf16[512,512]{1,0:T(8,128)(2,1)}, bf16[512,512]{1,0:T(8,128)(2,1)S(1)}, u32[]{:S(2)}, u32[]{:S(2)}) collective-permute-start(bf16[512,512]{1,0:T(8,128)(2,1)} %get-tuple-element.144), channel_id=1, source_target_pairs={{0,15},{1,14},{2,13},{3,12},{4,11},{5,10},{6,9},{7,8},{8,7},{9,6},... | collective-permute-start | bytes 1572872 | tf_op jit(solution)/shard_map/ppermute | solution.py:413
  181.1 2.5 %copy-start.13 = (bf16[512,512]{1,0:T(8,128)(2,1)}, bf16[512,512]{1,0:T(8,128)(2,1)S(1)}, u32[]{:S(2)}) copy-start(bf16[512,512]{1,0:T(8,128)(2,1)S(1)} %collective-permute-done.16.refs_0_) | copy-start | bytes 1572868
  183.6 0.8 copy-start.14
  183.6 1.0 copy-start.15
  205.1 0.8 copy-start.17
  217.9 0.8 copy-start.16

commit v2 on v1

--- a/solution.py
+++ b/solution.py
@@ -414,10 +414,10 @@
 
     far = list(range(shards // 2, shards))
     near = list(range(1, shards // 2))
-    near = near[:2] + near[:2:-1] + near[2:3]
-    first, second = far[:1], far[1:3] + near[:2]
-    late = [far[6 + i : 7 + i] + near[3 + 2 * i : 5 + 2 * i] for i in range(len(far) - 6)]
-    third = far[3:5] + far[5:6] + near[2:3] + [k for wave in late for k in wave] + [0]
+    near = near[:3] + near[:2:-1]
+    first, second = far[:1], far[1:3] + near[:3]
+    late = [far[6 + i : 7 + i] + near[4 + 2 * i : 6 + 2 * i] for i in range(len(far) - 6)]
+    third = far[3:5] + far[5:6] + near[3:4] + [k for wave in late for k in wave] + [0]
     ranks = first + second + third
     groups = [[0] + far[:2], far[2:3] + near[:2], far[3:4] + near[2:3]]
     groups += [far[4 + i : 5 + i] + near[3 + 2 * i : 5 + 2 * i] for i in range(len(far) - 4)]
@@ -457,7 +457,7 @@
     held.update(zip(first, chunks))
     depart(first)
     order = gather(second, jnp.zeros((8, 128), jnp.int32))
-    depart(far[1:2] + near[:2])
+    depart(far[1:2] + near[:3])
 
     seat = (here % inner)[None]
     rows = -(-shards * shards // slices)
@@ -473,9 +473,9 @@
     )
     order = release(carried, far[2:3])
     pieces, carried = summarize(
-        seat, live_rows, factors, begun, *weights, (steps - 1, steps, steps), inner, carry(order, far[0], *near[:2])
-    )
-    order = release(carried, [], far[0], *near[:2])
+        seat, live_rows, factors, begun, *weights, (steps - 1, steps, steps), inner, carry(order, far[0], *near[:3])
+    )
+    order = release(carried, [], far[0], *near[:3])
     parts = [pieces[0]] + [send(pieces[k], k) for k in range(1, inner)]
     piece = jax.ShapeDtypeStruct(parts[0].shape, jnp.bfloat16)
     (part,), carried = small_call(
@@ -501,7 +501,7 @@
     (mixed,), carried = small_call(
         join_kernel, "join", [seat] + parts, [mixed], carry(order), scalars=1, parts=inner
     )
-    order = release(carried, far[5:6] + near[2:3])
+    order = release(carried, far[5:6] + near[3:4])
 
     middle_t = entry_t[channels:]
     sources = here ^ jnp.array(ranks, jnp.int32)

time: 224 us -> 217 us (0.969)
  waiting for transfers between devices: 55 us -> 50.7 us
  starting transfers between devices: 43.3 us -> 40.1 us
    ppermute x24, waiting for transfers between devices: 55 us -> 50.7 us  [send(): return lax.ppermute(chunk, 'pts', [(i, i ^ k) for i in range(shards)])]
    ppermute x24, starting transfers between devices: 43.3 us -> 40.1 us  [send(): return lax.ppermute(chunk, 'pts', [(i, i ^ k) for i in range(shards)])]
    unnamed x48 -> x46, local copies, waits for them, and re-layouts: 7.05 us -> 6.65 us
  transfers between devices with their start and end apart: 24 -> 24, of which waited for: 9 -> 6; matrix products, arithmetic and copies ran while one was open for 1% -> 1% of each run, Pallas kernels for 47% -> 49%
where the time goes in v2:
time: 217 us; the launch traced here: 216 us
  Pallas kernels  117 us (54%)
  waiting for transfers between devices  50.7 us (23%)
  starting transfers between devices  40.1 us (18%)
  local copies, waits for them, and re-layouts  7.46 us (3%)
    pallas_call x7, Pallas kernels, finish(): pl.pallas_call(functools.partial(finish_kernel, ids, block_rows, len(kept...  57.9 us
    ppermute x24, waiting for transfers between devices, send(): return lax.ppermute(chunk, 'pts', [(i, i ^ k) for i in range(shards)])  50.7 us
    ppermute x24, starting transfers between devices, send(): return lax.ppermute(chunk, 'pts', [(i, i ^ k) for i in range(shards)])  40.1 us
    pallas_call x2, Pallas kernels, summarize(): pl.pallas_call(functools.partial(summary_kernel, pieces, steps[0], 2 * le...  33.1 us
    pallas_call x3, Pallas kernels, gather_blocks(): pl.pallas_call(functools.partial(gather_kernel, plan, offsets, per_peer,...  23.2 us
    unnamed x46, local copies, waits for them, and re-layouts  6.65 us
  transfers between devices with their start and end apart: 24, of which 6 were waited for; matrix products, arithmetic and copies ran while one was open for 1% of the time, Pallas kernels for 49%

profile of v2, /device:TPU:8, one launch (start us, length us, event | category | flops | bytes accessed | tf_op | source)
XLA Modules:
  0.0 215.9 jit_solution(15732133280336402355)
XLA Ops:
  0.7 0.7 copy-done.1
  1.4 0.7 copy-done.3
  2.1 4.7 %gather_blocks.3 = (s32[64]{0:T(128)S(1)}, s32[16]{0:T(128)S(1)}, bf16[512,512]{1,0:T(8,128)(2,1)}) custom-call(s32[1]{0:T(128)} %bitcast.2.here_ref, s32[1]{0:T(128)S(6)} %copy.117.refs_0_, s32[64]{0:T(128)S(1)} %copy-done.3, s32[64,128]{1,0:T(8,128)S(1)} %copy-done.1, bf16[64,128,512]{2,1,0:T(8,128)(2,1)} %bitcast.27), custom_call_target="tpu_custom_call" | custom-call | tf_op jit(solution)/shard_map/gather_blocks/pallas_call | solution.py:113
  6.7 2.7 %collective-permute-start = (bf16[512,512]{1,0:T(8,128)(2,1)}, bf16[512,512]{1,0:T(8,128)(2,1)S(1)}, u32[]{:S(2)}, u32[]{:S(2)}) collective-permute-start(bf16[512,512]{1,0:T(8,128)(2,1)} %get-tuple-element.88), channel_id=1, source_target_pairs={{0,8},{1,9},{2,10},{3,11},{4,12},{5,13},{6,14},{7,15},{8,0},{9,1},... | collective-permute-start | bytes 1572872 | tf_op jit(solution)/shard_map/ppermute | solution.py:413
  9.5 0.6 broadcast_in_dim.40.refs_3_
  10.1 6.9 %gather_blocks.4 = (s32[8,128]{1,0:T(8,128)}, bf16[512,512]{1,0:T(8,128)(2,1)}, bf16[512,512]{1,0:T(8,128)(2,1)}, bf16[512,512]{1,0:T(8,128)(2,1)}, bf16[512,512]{1,0:T(8,128)(2,1)}, /*index=5*/bf16[512,512]{1,0:T(8,128)(2,1)}) custom-call(s32[1]{0:T(128)} %bitcast.2.here_ref, s32[64]{0:T(128)S(1)} %get-tuple-element.83.refs_0_, ...), custom_call_target="tpu_custom_call", output_to_operand_aliasing={{0}: (4, {})} | custom-call | tf_op jit(solution)/shard_map/gather_blocks/pallas_call | solution.py:113
  17.0 1.6 collective-permute-start.1
  18.6 1.4 collective-permute-start.2
  20.0 0.5 collective-permute-start.3
  20.5 1.3 collective-permute-start.7
  22.3 1.5 copy.62
  23.9 31.6 %summarize.2 = (s32[8,128]{1,0:T(8,128)}, bf16[512,512]{1,0:T(8,128)(2,1)}, f32[8,80,256]{2,1,0:T(8,128)S(1)}) custom-call(s32[1]{0:T(128)} %bitcast.1.seat_ref, s32[1]{0:T(128)S(6)} %mul.3.live_ref, f32[8]{0:T(128)S(1)} %broadcast_divide_fusion.factor_ref, f32[8,128]{1,0:T(8,128)S(1)} %broadcast_in_dim.35.before_ref, ...), custom_call_target="tpu_custom_call", output_to_operand_aliasing={{0}: (8, {}), {1}: (9, {})} | custom-call | tf_op jit(solution)/shard_map/summarize/pallas_call | solution.py:203
  55.5 3.5 %collective-permute-start.11 = (bf16[512,512]{1,0:T(8,128)(2,1)}, bf16[512,512]{1,0:T(8,128)(2,1)S(1)}, u32[]{:S(2)}, u32[]{:S(2)}) collective-permute-start(bf16[512,512]{1,0:T(8,128)(2,1)} %get-tuple-element.110), channel_id=1, source_target_pairs={{0,10},{1,11},{2,8},{3,9},{4,14},{5,15},{6,12},{7,13},{8,2},{9,3},... | collective-permute-start | bytes 1572872 | tf_op jit(solution)/shard_map/ppermute | solution.py:413
  59.0 1.5 summarize.3
  60.5 5.0 %collective-permute-start.4 = (bf16[2,80,256]{2,1,0:T(8,128)(2,1)S(1)}, bf16[2,80,256]{2,1,0:T(8,128)(2,1)S(1)}, u32[]{:S(2)}, u32[]{:S(2)}) collective-permute-start(bf16[2,80,256]{2,1,0:T(8,128)(2,1)S(1)} %get-tuple-element.93), channel_id=1, source_target_pairs={{0,1},{1,0},{2,3},{3,2},{4,5},{5,4},{6,7},{7,6},{8,9},{9,8},{10,11... | collective-permute-start | bytes 245768 | tf_op jit(solution)/shard_map/ppermute | solution.py:413
  65.5 0.4 collective-permute-start.5
  66.0 1.1 collective-permute-start.6
  67.1 0.9 collective-permute-done.4.refs_1_
  68.0 5.4 %collective-permute-done.5.refs_2_ = bf16[2,80,256]{2,1,0:T(8,128)(2,1)S(1)} collective-permute-done((bf16[2,80,256]{2,1,0:T(8,128)(2,1)S(1)}, bf16[2,80,256]{2,1,0:T(8,128)(2,1)S(1)}, u32[]{:S(2)}, u32[]{:S(2)}) %collective-permute-start.5) | collective-permute-done | bytes 81952 | tf_op jit(solution)/shard_map/ppermute | solution.py:413
  73.4 1.7 collective-permute-start.10
  75.1 1.9 collective-permute-start.8
  77.2 11.6 %gather_blocks.5 = (s32[8,128]{1,0:T(8,128)}, bf16[512,512]{1,0:T(8,128)(2,1)}, bf16[512,512]{1,0:T(8,128)(2,1)}, bf16[512,512]{1,0:T(8,128)(2,1)}, bf16[512,512...) custom-call(s32[1]{0:T(128)} %bitcast.2.here_ref, ...), custom_call_target="tpu_custom_call", output_to_operand_aliasing={{0}: (4, {})} | custom-call | tf_op jit(solution)/shard_map/gather_blocks/pallas_call | solution.py:113
  88.9 0.8 copy-done.6
  89.7 2.3 %attend.1 = (s32[8,128]{1,0:T(8,128)}, bf16[512,512]{1,0:T(8,128)(2,1)}, bf16[512,512]{1,0:T(8,128)(2,1)}, bf16[512,512]{1,0:T(8,128)(2,1)}, bf16[512,512]{1,0:T...) custom-call(bf16[192,64]{1,0:T(8,128)(2,1)S(1)} %bitcast.19, ...), custom_call_target="tpu_custom_call", output_to_operand_aliasing={{0}: (5, {}), {1}: (6, {}), {2}: (7, {}), {3}: (8, {}), {4}... | custom-call | tf_op jit(solution)/shard_map/attend/pallas_call | solution.py:240
  92.0 1.5 collective-permute-start.14
  93.5 0.5 collective-permute-start.13
  94.0 1.5 collective-permute-start.12
  95.8 1.6 collective-permute-start.20
  97.4 2.6 %collective-permute-start.23 = (bf16[512,512]{1,0:T(8,128)(2,1)}, bf16[512,512]{1,0:T(8,128)(2,1)S(1)}, u32[]{:S(2)}, u32[]{:S(2)}) collective-permute-start(bf16[512,512]{1,0:T(8,128)(2,1)} %get-tuple-element.146), channel_id=1, source_target_pairs={{0,11},{1,10},{2,9},{3,8},{4,15},{5,14},{6,13},{7,12},{8,3},{9,2},... | collective-permute-start | bytes 1572872 | tf_op jit(solution)/shard_map/ppermute | solution.py:413
  100.0 1.2 collective-permute-start.21
  101.2 10.1 %finish.7 = (s32[8,128]{1,0:T(8,128)}, bf16[512,512]{1,0:T(8,128)(2,1)}, bf16[512,512]{1,0:T(8,128)(2,1)}, bf16[512,512]{1,0:T(8,128)(2,1)}, bf16[512,512]{1,0:T...) custom-call(s32[16]{0:T(128)S(1)} %broadcast_xor_fusion.place_ref, ...), custom_call_target="tpu_custom_call", output_to_operand_aliasing={{0}: (10, {}), {1}: (11, {}), {2}: (12, {}), {3}: (13, {}),... | custom-call | tf_op jit(solution)/shard_map/finish/pallas_call | solution.py:359
  111.4 2.0 collective-permute-start.22
  113.4 1.3 collective-permute-start.17
  114.7 10.1 %finish.8 = (s32[8,128]{1,0:T(8,128)}, bf16[512,512]{1,0:T(8,128)(2,1)}, bf16[512,512]{1,0:T(8,128)(2,1)}, bf16[8192,512]{1,0:T(8,128)(2,1)}) custom-call(s32[16]{0:T(128)S(1)} %broadcast_xor_fusion.place_ref, s32[16]{0:T(128)S(1)} %bitcast.21, ...), custom_call_target="tpu_custom_call", output_to_operand_aliasing={{0}: (10, {}), {1}: (11, {}), {2}: (12, {}), {3}: (13, {})} | custom-call | tf_op jit(solution)/shard_map/finish/pallas_call | solution.py:359
  124.9 6.7 %collective-permute-done.20.refs_0_ = bf16[512,512]{1,0:T(8,128)(2,1)S(1)} collective-permute-done((bf16[512,512]{1,0:T(8,128)(2,1)}, bf16[512,512]{1,0:T(8,128)(2,1)S(1)}, u32[]{:S(2)}, u32[]{:S(2)}) %collective-permute-start.20) | collective-permute-done | bytes 524320 | tf_op jit(solution)/shard_map/ppermute | solution.py:413
  131.6 12.3 %collective-permute-done.23.refs_0_ = bf16[512,512]{1,0:T(8,128)(2,1)S(1)} collective-permute-done((bf16[512,512]{1,0:T(8,128)(2,1)}, bf16[512,512]{1,0:T(8,128)(2,1)S(1)}, u32[]{:S(2)}, u32[]{:S(2)}) %collective-permute-start.23) | collective-permute-done | bytes 524320 | tf_op jit(solution)/shard_map/ppermute | solution.py:413
  143.9 3.7 %collective-permute-start.18 = (bf16[512,512]{1,0:T(8,128)(2,1)S(1)}, bf16[512,512]{1,0:T(8,128)(2,1)S(1)}, u32[]{:S(2)}, u32[]{:S(2)}) collective-permute-start(bf16[512,512]{1,0:T(8,128)(2,1)S(1)} %copy-done.5), channel_id=1, source_target_pairs={{0,5},{1,4},{2,7},{3,6},{4,1},{5,0},{6,3},{7,2},{8,13},{9,12},{10,... | collective-permute-start | bytes 1572872 | tf_op jit(solution)/shard_map/ppermute | solution.py:413
  147.5 2.5 %collective-permute-start.16 = (bf16[512,512]{1,0:T(8,128)(2,1)S(1)}, bf16[512,512]{1,0:T(8,128)(2,1)S(1)}, u32[]{:S(2)}, u32[]{:S(2)}) collective-permute-start(bf16[512,512]{1,0:T(8,128)(2,1)S(1)} %copy-done.4), channel_id=1, source_target_pairs={{0,14},{1,15},{2,12},{3,13},{4,10},{5,11},{6,8},{7,9},{8,6},{9,7},... | collective-permute-start | bytes 1572872 | tf_op jit(solution)/shard_map/ppermute | solution.py:413
  150.5 7.5 %finish.9 = (s32[8,128]{1,0:T(8,128)}, bf16[8192,512]{1,0:T(8,128)(2,1)}) custom-call(s32[16]{0:T(128)S(1)} %broadcast_xor_fusion.place_ref, s32[16]{0:T(128)S(1)} %bitcast.22, f32[8]{0:T(128)S(1)} %broadcast_divide_fusion.factor_ref, bf16[512,512]{1,0:T(8,128)(2,1)} %copy-done.9, ...), custom_call_target="tpu_custom_call", output_to_operand_aliasing={{0}: (9, {}), {1}: (10, {})} | custom-call | tf_op jit(solution)/shard_map/finish/pallas_call | solution.py:359
  158.0 10.4 %finish.10 = (s32[8,128]{1,0:T(8,128)}, bf16[8192,512]{1,0:T(8,128)(2,1)}) custom-call(s32[16]{0:T(128)S(1)} %broadcast_xor_fusion.place_ref, s32[16]{0:T(128)S(1)} %bitcast.23, f32[8]{0:T(128)S(1)} %broadcast_divide_fusion.factor_ref, bf16[512,512]{1,0:T(8,128)(2,1)} %copy-done.8, ...), custom_call_target="tpu_custom_call", output_to_operand_aliasing={{0}: (10, {}), {1}: (11, {})} | custom-call | tf_op jit(solution)/shard_map/finish/pallas_call | solution.py:359
  168.4 11.7 %collective-permute-done.18.refs_1_ = bf16[512,512]{1,0:T(8,128)(2,1)S(1)} collective-permute-done((bf16[512,512]{1,0:T(8,128)(2,1)S(1)}, bf16[512,512]{1,0:T(8,128)(2,1)S(1)}, u32[]{:S(2)}, u32[]{:S(2)}) %collective-permute-start.18) | collective-permute-done | bytes 524320 | tf_op jit(solution)/shard_map/ppermute | solution.py:413
  180.1 0.8 copy-done.14
  180.9 10.1 %finish.11 = (s32[8,128]{1,0:T(8,128)}, bf16[8192,512]{1,0:T(8,128)(2,1)}) custom-call(s32[16]{0:T(128)S(1)} %broadcast_xor_fusion.place_ref, s32[16]{0:T(128)S(1)} %bitcast.24, f32[8]{0:T(128)S(1)} %broadcast_divide_fusion.factor_ref, bf16[512,512]{1,0:T(8,128)(2,1)} %copy-done.11, ...), custom_call_target="tpu_custom_call", output_to_operand_aliasing={{0}: (10, {}), {1}: (11, {})} | custom-call | tf_op jit(solution)/shard_map/finish/pallas_call | solution.py:359
  191.1 0.8 copy-done.16
  191.9 4.8 %finish.12 = (s32[8,128]{1,0:T(8,128)}, bf16[8192,512]{1,0:T(8,128)(2,1)}) custom-call(s32[16]{0:T(128)S(1)} %broadcast_xor_fusion.place_ref, s32[16]{0:T(128)S(1)} %bitcast.25, f32[8]{0:T(128)S(1)} %broadcast_divide_fusion.factor_ref, bf16[512,512]{1,0:T(8,128)(2,1)} %copy-done.16, ...), custom_call_target="tpu_custom_call", output_to_operand_aliasing={{0}: (8, {}), {1}: (9, {})} | custom-call | tf_op jit(solution)/shard_map/finish/pallas_call | solution.py:359
  196.7 13.6 %collective-permute-done.15.refs_0_ = bf16[512,512]{1,0:T(8,128)(2,1)S(1)} collective-permute-done((bf16[512,512]{1,0:T(8,128)(2,1)}, bf16[512,512]{1,0:T(8,128)(2,1)S(1)}, u32[]{:S(2)}, u32[]{:S(2)}) %collective-permute-start.15) | collective-permute-done | bytes 524320 | tf_op jit(solution)/shard_map/ppermute | solution.py:413
  210.3 0.8 copy-done.15
  211.1 4.8 %finish.13 = (s32[8,128]{1,0:T(8,128)}, bf16[8192,512]{1,0:T(8,128)(2,1)}) custom-call(s32[16]{0:T(128)S(1)} %broadcast_xor_fusion.place_ref, s32[16]{0:T(128)S(1)} %bitcast.26, f32[8]{0:T(128)S(1)} %broadcast_divide_fusion.factor_ref, bf16[512,512]{1,0:T(8,128)(2,1)} %copy-done.15, ...), custom_call_target="tpu_custom_call", output_to_operand_aliasing={{0}: (8, {}), {1}: (9, {})} | custom-call | tf_op jit(solution)/shard_map/finish/pallas_call | solution.py:359
  (73 shorter events, 1.5 us)
Async XLA Ops:
  0.7 0.8 copy-start.1
  1.4 0.7 copy-start.3
  2.1 8.0 %copy-start.2 = (s32[64,128]{1,0:T(8,128)S(1)}, s32[64,128]{1,0:T(8,128)}, u32[]{:S(2)}) copy-start(s32[64,128]{1,0:T(8,128)} %refs_1_.5) | copy-start | bytes 98308
  2.1 19.9 %copy-start.17 = (bf16[8,64,256]{2,1,0:T(8,128)(2,1)S(1)}, bf16[8,64,256]{2,1,0:T(8,128)(2,1)}, u32[]{:S(2)}) copy-start(bf16[8,64,256]{2,1,0:T(8,128)(2,1)} %param.16) | copy-start | bytes 786436
  2.1 21.8 %copy-start.19 = (f32[8]{0:T(128)S(1)}, f32[8]{0:T(128)}, u32[]{:S(2)}) copy-start(f32[8]{0:T(128)} %param.14) | copy-start | bytes 100
  6.7 48.7 %collective-permute-start = (bf16[512,512]{1,0:T(8,128)(2,1)}, bf16[512,512]{1,0:T(8,128)(2,1)S(1)}, u32[]{:S(2)}, u32[]{:S(2)}) collective-permute-start(bf16[512,512]{1,0:T(8,128)(2,1)} %get-tuple-element.88), channel_id=1, source_target_pairs={{0,8},{1,9},{2,10},{3,11},{4,12},{5,13},{6,14},{7,15},{8,0},{9,1},... | collective-permute-start | bytes 1572872 | tf_op jit(solution)/shard_map/ppermute | solution.py:413
  17.0 42.0 %collective-permute-start.1 = (bf16[512,512]{1,0:T(8,128)(2,1)}, bf16[512,512]{1,0:T(8,128)(2,1)}, u32[]{:S(2)}, u32[]{:S(2)}) collective-permute-start(bf16[512,512]{1,0:T(8,128)(2,1)} %get-tuple-element.89), channel_id=1, source_target_pairs={{0,1},{1,0},{2,3},{3,2},{4,5},{5,4},{6,7},{7,6},{8,9},{9,8},{10,11... | collective-permute-start | bytes 1572872 | tf_op jit(solution)/shard_map/ppermute | solution.py:413
  18.6 40.3 %collective-permute-start.2 = (bf16[512,512]{1,0:T(8,128)(2,1)}, bf16[512,512]{1,0:T(8,128)(2,1)}, u32[]{:S(2)}, u32[]{:S(2)}) collective-permute-start(bf16[512,512]{1,0:T(8,128)(2,1)} %get-tuple-element.90), channel_id=1, source_target_pairs={{0,2},{1,3},{2,0},{3,1},{4,6},{5,7},{6,4},{7,5},{8,10},{9,11},{10,... | collective-permute-start | bytes 1572872 | tf_op jit(solution)/shard_map/ppermute | solution.py:413
  20.0 39.0 %collective-permute-start.3 = (bf16[512,512]{1,0:T(8,128)(2,1)}, bf16[512,512]{1,0:T(8,128)(2,1)}, u32[]{:S(2)}, u32[]{:S(2)}) collective-permute-start(bf16[512,512]{1,0:T(8,128)(2,1)} %get-tuple-element.91), channel_id=1, source_target_pairs={{0,3},{1,2},{2,1},{3,0},{4,7},{5,6},{6,5},{7,4},{8,11},{9,10},{10,... | collective-permute-start | bytes 1572872 | tf_op jit(solution)/shard_map/ppermute | solution.py:413
  20.5 46.5 %collective-permute-start.7 = (bf16[512,512]{1,0:T(8,128)(2,1)}, bf16[512,512]{1,0:T(8,128)(2,1)}, u32[]{:S(2)}, u32[]{:S(2)}) collective-permute-start(bf16[512,512]{1,0:T(8,128)(2,1)} %get-tuple-element.97), channel_id=1, source_target_pairs={{0,9},{1,8},{2,11},{3,10},{4,13},{5,12},{6,15},{7,14},{8,1},{9,0},... | collective-permute-start | bytes 1572872 | tf_op jit(solution)/shard_map/ppermute | solution.py:413
  55.4 21.6 %copy-start.20 = (s32[16]{0:T(128)S(1)}, s32[16]{0:T(128)}, u32[]{:S(2)}) copy-start(s32[16]{0:T(128)} %constant.30.clone) | copy-start | bytes 196
  55.4 21.6 %copy-start.18 = (bf16[64,192]{1,0:T(8,128)(2,1)S(1)}, bf16[64,192]{1,0:T(8,128)(2,1)}, u32[]{:S(2)}) copy-start(bf16[64,192]{1,0:T(8,128)(2,1)} %param.17) | copy-start | bytes 73732
  55.5 3.5 %copy-start.7 = (bf16[512,512]{1,0:T(8,128)(2,1)}, bf16[512,512]{1,0:T(8,128)(2,1)S(1)}, u32[]{:S(2)}) copy-start(bf16[512,512]{1,0:T(8,128)(2,1)S(1)} %collective-permute-done.refs_1_) | copy-start | bytes 1572868
  55.5 33.3 %collective-permute-start.11 = (bf16[512,512]{1,0:T(8,128)(2,1)}, bf16[512,512]{1,0:T(8,128)(2,1)S(1)}, u32[]{:S(2)}, u32[]{:S(2)}) collective-permute-start(bf16[512,512]{1,0:T(8,128)(2,1)} %get-tuple-element.110), channel_id=1, source_target_pairs={{0,10},{1,11},{2,8},{3,9},{4,14},{5,15},{6,12},{7,13},{8,2},{9,3},... | collective-permute-start | bytes 1572872 | tf_op jit(solution)/shard_map/ppermute | solution.py:413
  60.5 7.4 %collective-permute-start.4 = (bf16[2,80,256]{2,1,0:T(8,128)(2,1)S(1)}, bf16[2,80,256]{2,1,0:T(8,128)(2,1)S(1)}, u32[]{:S(2)}, u32[]{:S(2)}) collective-permute-start(bf16[2,80,256]{2,1,0:T(8,128)(2,1)S(1)} %get-tuple-element.93), channel_id=1, source_target_pairs={{0,1},{1,0},{2,3},{3,2},{4,5},{5,4},{6,7},{7,6},{8,9},{9,8},{10,11... | collective-permute-start | bytes 245768 | tf_op jit(solution)/shard_map/ppermute | solution.py:413
  65.5 7.8 %collective-permute-start.5 = (bf16[2,80,256]{2,1,0:T(8,128)(2,1)S(1)}, bf16[2,80,256]{2,1,0:T(8,128)(2,1)S(1)}, u32[]{:S(2)}, u32[]{:S(2)}) collective-permute-start(bf16[2,80,256]{2,1,0:T(8,128)(2,1)S(1)} %get-tuple-element.94), channel_id=1, source_target_pairs={{0,2},{1,3},{2,0},{3,1},{4,6},{5,7},{6,4},{7,5},{8,10},{9,11},{10,... | collective-permute-start | bytes 245768 | tf_op jit(solution)/shard_map/ppermute | solution.py:413
  66.0 7.4 %collective-permute-start.6 = (bf16[2,80,256]{2,1,0:T(8,128)(2,1)S(1)}, bf16[2,80,256]{2,1,0:T(8,128)(2,1)S(1)}, u32[]{:S(2)}, u32[]{:S(2)}) collective-permute-start(bf16[2,80,256]{2,1,0:T(8,128)(2,1)S(1)} %get-tuple-element.95), channel_id=1, source_target_pairs={{0,3},{1,2},{2,1},{3,0},{4,7},{5,6},{6,5},{7,4},{8,11},{9,10},{10,... | collective-permute-start | bytes 245768 | tf_op jit(solution)/shard_map/ppermute | solution.py:413
  73.4 15.4 %collective-permute-start.10 = (bf16[2,80,256]{2,1,0:T(8,128)(2,1)S(1)}, bf16[2,80,256]{2,1,0:T(8,128)(2,1)S(1)}, u32[]{:S(2)}, u32[]{:S(2)}) collective-permute-start(bf16[2,80,256]{2,1,0:T(8,128)(2,1)S(1)} %get-tuple-element.98.refs_1_), channel_id=1, source_target_pairs={{0,12},{1,13},{2,14},{3,15},{4,8},{5,9},{6,10},{7,11},{8,4},{9,5},... | collective-permute-start | bytes 245768 | tf_op jit(solution)/shard_map/ppermute | solution.py:413
  75.1 13.7 %collective-permute-start.9 = (bf16[2,80,256]{2,1,0:T(8,128)(2,1)S(1)}, bf16[2,80,256]{2,1,0:T(8,128)(2,1)S(1)}, u32[]{:S(2)}, u32[]{:S(2)}) collective-permute-start(bf16[2,80,256]{2,1,0:T(8,128)(2,1)S(1)} %get-tuple-element.98.refs_1_), channel_id=1, source_target_pairs={{0,8},{1,9},{2,10},{3,11},{4,12},{5,13},{6,14},{7,15},{8,0},{9,1},... | collective-permute-start | bytes 245768 | tf_op jit(solution)/shard_map/ppermute | solution.py:413
  75.1 13.7 %collective-permute-start.8 = (bf16[2,80,256]{2,1,0:T(8,128)(2,1)S(1)}, bf16[2,80,256]{2,1,0:T(8,128)(2,1)S(1)}, u32[]{:S(2)}, u32[]{:S(2)}) collective-permute-start(bf16[2,80,256]{2,1,0:T(8,128)(2,1)S(1)} %get-tuple-element.98.refs_1_), channel_id=1, source_target_pairs={{0,4},{1,5},{2,6},{3,7},{4,0},{5,1},{6,2},{7,3},{8,12},{9,13},{10,... | collective-permute-start | bytes 245768 | tf_op jit(solution)/shard_map/ppermute | solution.py:413
  77.1 24.1 %copy-start = (bf16[512,512]{1,0:T(8,128)(2,1)S(1)}, bf16[512,512]{1,0:T(8,128)(2,1)}, u32[]{:S(2)}) copy-start(bf16[512,512]{1,0:T(8,128)(2,1)} %refs_4_.3) | copy-start | bytes 1572868
  88.8 0.9 copy-start.6
  92.0 8.0 %collective-permute-start.14 = (bf16[2,64,256]{2,1,0:T(8,128)(2,1)S(1)}, bf16[2,64,256]{2,1,0:T(8,128)(2,1)S(1)}, u32[]{:S(2)}, u32[]{:S(2)}) collective-permute-start(bf16[2,64,256]{2,1,0:T(8,128)(2,1)S(1)} %get-tuple-element.115.refs_0_), channel_id=1, source_target_pairs={{0,3},{1,2},{2,1},{3,0},{4,7},{5,6},{6,5},{7,4},{8,11},{9,10},{10,... | collective-permute-start | bytes 196616 | tf_op jit(solution)/shard_map/ppermute | solution.py:413
  93.5 6.5 %collective-permute-start.13 = (bf16[2,64,256]{2,1,0:T(8,128)(2,1)S(1)}, bf16[2,64,256]{2,1,0:T(8,128)(2,1)S(1)}, u32[]{:S(2)}, u32[]{:S(2)}) collective-permute-start(bf16[2,64,256]{2,1,0:T(8,128)(2,1)S(1)} %get-tuple-element.115.refs_0_), channel_id=1, source_target_pairs={{0,2},{1,3},{2,0},{3,1},{4,6},{5,7},{6,4},{7,5},{8,10},{9,11},{10,... | collective-permute-start | bytes 196616 | tf_op jit(solution)/shard_map/ppermute | solution.py:413
  94.0 6.0 %collective-permute-start.12 = (bf16[2,64,256]{2,1,0:T(8,128)(2,1)S(1)}, bf16[2,64,256]{2,1,0:T(8,128)(2,1)S(1)}, u32[]{:S(2)}, u32[]{:S(2)}) collective-permute-start(bf16[2,64,256]{2,1,0:T(8,128)(2,1)S(1)} %get-tuple-element.115.refs_0_), channel_id=1, source_target_pairs={{0,1},{1,0},{2,3},{3,2},{4,5},{5,4},{6,7},{7,6},{8,9},{9,8},{10,11... | collective-permute-start | bytes 196616 | tf_op jit(solution)/shard_map/ppermute | solution.py:413
  95.8 35.8 %collective-permute-start.20 = (bf16[512,512]{1,0:T(8,128)(2,1)}, bf16[512,512]{1,0:T(8,128)(2,1)S(1)}, u32[]{:S(2)}, u32[]{:S(2)}) collective-permute-start(bf16[512,512]{1,0:T(8,128)(2,1)} %get-tuple-element.143), channel_id=1, source_target_pairs={{0,12},{1,13},{2,14},{3,15},{4,8},{5,9},{6,10},{7,11},{8,4},{9,5},... | collective-permute-start | bytes 1572872 | tf_op jit(solution)/shard_map/ppermute | solution.py:413
  97.4 46.4 %collective-permute-start.23 = (bf16[512,512]{1,0:T(8,128)(2,1)}, bf16[512,512]{1,0:T(8,128)(2,1)S(1)}, u32[]{:S(2)}, u32[]{:S(2)}) collective-permute-start(bf16[512,512]{1,0:T(8,128)(2,1)} %get-tuple-element.146), channel_id=1, source_target_pairs={{0,11},{1,10},{2,9},{3,8},{4,15},{5,14},{6,13},{7,12},{8,3},{9,2},... | collective-permute-start | bytes 1572872 | tf_op jit(solution)/shard_map/ppermute | solution.py:413
  100.0 47.5 %collective-permute-start.21 = (bf16[512,512]{1,0:T(8,128)(2,1)}, bf16[512,512]{1,0:T(8,128)(2,1)S(1)}, u32[]{:S(2)}, u32[]{:S(2)}) collective-permute-start(bf16[512,512]{1,0:T(8,128)(2,1)} %get-tuple-element.144), channel_id=1, source_target_pairs={{0,7},{1,6},{2,5},{3,4},{4,3},{5,2},{6,1},{7,0},{8,15},{9,14},{10,... | collective-permute-start | bytes 1572872 | tf_op jit(solution)/shard_map/ppermute | solution.py:413
  111.4 32.5 %copy-start.5 = (bf16[512,512]{1,0:T(8,128)(2,1)S(1)}, bf16[512,512]{1,0:T(8,128)(2,1)}, u32[]{:S(2)}) copy-start(bf16[512,512]{1,0:T(8,128)(2,1)} %get-tuple-element.141) | copy-start | bytes 1572868
  111.4 36.2 %copy-start.4 = (bf16[512,512]{1,0:T(8,128)(2,1)S(1)}, bf16[512,512]{1,0:T(8,128)(2,1)}, u32[]{:S(2)}) copy-start(bf16[512,512]{1,0:T(8,128)(2,1)} %get-tuple-element.139) | copy-start | bytes 1572868
  111.4 38.7 %collective-permute-start.22 = (bf16[512,512]{1,0:T(8,128)(2,1)}, bf16[512,512]{1,0:T(8,128)(2,1)S(1)}, u32[]{:S(2)}, u32[]{:S(2)}) collective-permute-start(bf16[512,512]{1,0:T(8,128)(2,1)} %get-tuple-element.145), channel_id=1, source_target_pairs={{0,6},{1,7},{2,4},{3,5},{4,2},{5,3},{6,0},{7,1},{8,14},{9,15},{10,... | collective-permute-start | bytes 1572872 | tf_op jit(solution)/shard_map/ppermute | solution.py:413
  113.4 54.9 %collective-permute-start.17 = (bf16[512,512]{1,0:T(8,128)(2,1)}, bf16[512,512]{1,0:T(8,128)(2,1)S(1)}, u32[]{:S(2)}, u32[]{:S(2)}) collective-permute-start(bf16[512,512]{1,0:T(8,128)(2,1)} %get-tuple-element.140), channel_id=1, source_target_pairs={{0,13},{1,12},{2,15},{3,14},{4,9},{5,8},{6,11},{7,10},{8,5},{9,4},... | collective-permute-start | bytes 1572872 | tf_op jit(solution)/shard_map/ppermute | solution.py:413
  131.6 26.4 %copy-start.8 = (bf16[512,512]{1,0:T(8,128)(2,1)}, bf16[512,512]{1,0:T(8,128)(2,1)S(1)}, u32[]{:S(2)}) copy-start(bf16[512,512]{1,0:T(8,128)(2,1)S(1)} %collective-permute-done.20.refs_0_) | copy-start | bytes 1572868
  131.6 36.8 %collective-permute-start.19 = (bf16[512,512]{1,0:T(8,128)(2,1)}, bf16[512,512]{1,0:T(8,128)(2,1)S(1)}, u32[]{:S(2)}, u32[]{:S(2)}) collective-permute-start(bf16[512,512]{1,0:T(8,128)(2,1)} %get-tuple-element.142), channel_id=1, source_target_pairs={{0,4},{1,5},{2,6},{3,7},{4,0},{5,1},{6,2},{7,3},{8,12},{9,13},{10,... | collective-permute-start | bytes 1572872 | tf_op jit(solution)/shard_map/ppermute | solution.py:413
  143.9 6.6 %copy-start.9 = (bf16[512,512]{1,0:T(8,128)(2,1)}, bf16[512,512]{1,0:T(8,128)(2,1)S(1)}, u32[]{:S(2)}) copy-start(bf16[512,512]{1,0:T(8,128)(2,1)S(1)} %collective-permute-done.23.refs_0_) | copy-start | bytes 1572868
  143.9 36.3 %collective-permute-start.18 = (bf16[512,512]{1,0:T(8,128)(2,1)S(1)}, bf16[512,512]{1,0:T(8,128)(2,1)S(1)}, u32[]{:S(2)}, u32[]{:S(2)}) collective-permute-start(bf16[512,512]{1,0:T(8,128)(2,1)S(1)} %copy-done.5), channel_id=1, source_target_pairs={{0,5},{1,4},{2,7},{3,6},{4,1},{5,0},{6,3},{7,2},{8,13},{9,12},{10,... | collective-permute-start | bytes 1572872 | tf_op jit(solution)/shard_map/ppermute | solution.py:413
  147.5 10.4 %copy-start.10 = (bf16[512,512]{1,0:T(8,128)(2,1)}, bf16[512,512]{1,0:T(8,128)(2,1)S(1)}, u32[]{:S(2)}) copy-start(bf16[512,512]{1,0:T(8,128)(2,1)S(1)} %collective-permute-done.21.refs_1_) | copy-start | bytes 1572868
  147.5 43.5 %collective-permute-start.16 = (bf16[512,512]{1,0:T(8,128)(2,1)S(1)}, bf16[512,512]{1,0:T(8,128)(2,1)S(1)}, u32[]{:S(2)}, u32[]{:S(2)}) collective-permute-start(bf16[512,512]{1,0:T(8,128)(2,1)S(1)} %copy-done.4), channel_id=1, source_target_pairs={{0,14},{1,15},{2,12},{3,13},{4,10},{5,11},{6,8},{7,9},{8,6},{9,7},... | collective-permute-start | bytes 1572872 | tf_op jit(solution)/shard_map/ppermute | solution.py:413
  150.1 7.9 %copy-start.12 = (bf16[512,512]{1,0:T(8,128)(2,1)}, bf16[512,512]{1,0:T(8,128)(2,1)S(1)}, u32[]{:S(2)}) copy-start(bf16[512,512]{1,0:T(8,128)(2,1)S(1)} %collective-permute-done.22.refs_2_) | copy-start | bytes 1572868
  150.1 60.2 %collective-permute-start.15 = (bf16[512,512]{1,0:T(8,128)(2,1)}, bf16[512,512]{1,0:T(8,128)(2,1)S(1)}, u32[]{:S(2)}, u32[]{:S(2)}) collective-permute-start(bf16[512,512]{1,0:T(8,128)(2,1)} %get-tuple-element.138), channel_id=1, source_target_pairs={{0,15},{1,14},{2,13},{3,12},{4,11},{5,10},{6,9},{7,8},{8,7},{9,6},... | collective-permute-start | bytes 1572872 | tf_op jit(solution)/shard_map/ppermute | solution.py:413
  168.4 11.8 %copy-start.11 = (bf16[512,512]{1,0:T(8,128)(2,1)}, bf16[512,512]{1,0:T(8,128)(2,1)S(1)}, u32[]{:S(2)}) copy-start(bf16[512,512]{1,0:T(8,128)(2,1)S(1)} %collective-permute-done.17.refs_0_) | copy-start | bytes 1572868
  168.4 11.8 %copy-start.13 = (bf16[512,512]{1,0:T(8,128)(2,1)}, bf16[512,512]{1,0:T(8,128)(2,1)S(1)}, u32[]{:S(2)}) copy-start(bf16[512,512]{1,0:T(8,128)(2,1)S(1)} %collective-permute-done.19.refs_2_) | copy-start | bytes 1572868
  180.1 0.8 copy-start.14
  191.1 0.8 copy-start.16
  210.3 0.8 copy-start.15
